TPU v7x, 256 devices: a whole 4x4x8 slice. The times are simulated.
256 devices in a mesh: section: 8 (over x, y_lo), expert: 16 (over y_hi, z), dp: 2 (over core).
Axes of the slice: x: 4, y: 4 (y_hi: 2, y_lo: 2; y = y_hi * 2 + y_lo), z: 8, core: 2. Of those that a mesh axis runs over, the one named last changes fastest.
Arguments:
- saved_rows: bfloat16 [8, 4096, 4096], P('section', ('expert', 'dp')), may hold values from -6 to 6
- grad_out: bfloat16 [8, 4096, 4096], P('section', ('expert', 'dp')), may hold values from -6 to 6
- expert_ids: int32 [8, 4096, 1], P('section', ('expert', 'dp')), may hold values from 0 to 3; in each aligned block of 128 rows (0 to 127, 128 to 255, ..., all dimensions but the last counted through in order) at most 48 rows name the same one
- combine: float32 [8, 4096, 1], P('section', ('expert', 'dp')), may hold values from 0.25 to 1
- w_gate: bfloat16 [8, 4096, 6144], P('section', 'dp', 'expert'), may hold values from -0.09375 to 0.09375
- w_up: bfloat16 [8, 4096, 6144], P('section', 'dp', 'expert'), may hold values from -0.09375 to 0.09375
- w_down: bfloat16 [8, 6144, 4096], P('section', 'expert', 'dp'), may hold values from -0.15625 to 0.15625
Outputs:
- grad_in: bfloat16 [8, 4096, 4096], P('section', ('expert', 'dp'))
- grad_gate: bfloat16 [8, 4096, 6144], P('section', 'dp', 'expert')
- grad_up: bfloat16 [8, 4096, 6144], P('section', 'dp', 'expert')
- grad_down: bfloat16 [8, 6144, 4096], P('section', 'expert', 'dp')
Inputs may be any that keep to these rules, and one draw needn't show every extreme that they name: `expert_ids`: within the 128 rows of one device no expert is chosen more than 48 times, and in every draw some device's rows choose one expert exactly 48 times.
All inputs are finite; a program needn't handle non-finite values.
Results may differ from a plain program's by a relative error of at most 0.0065.
Values may be sent and summed in bfloat16 or wider, within the bound.
A program may use at most 128 MiB of HBM per device.

v0:
```python
import jax
import jax.numpy as jnp
from jax import lax
from jax.sharding import PartitionSpec as P

EXPERTS = 4
CAP = 48


block_rows = 128


def swapped(x, axis, stride):
    return lax.ppermute(x, axis, [(i, i ^ 1 << stride) for i in range(lax.axis_size(axis))])


def contract(left_mat, right_mat, left_dim, right_dim):
    return lax.dot_general(
        left_mat,
        right_mat,
        (((left_dim,), (right_dim,)), ((), ())),
        preferred_element_type=jnp.float32,
    )


def rows_backward(rows_in, rows_grad, gate_mat, up_mat, down_mat):
    gate_proj = jnp.dot(rows_in, gate_mat, preferred_element_type=jnp.float32)
    up_proj = jnp.dot(rows_in, up_mat, preferred_element_type=jnp.float32)
    back_grad = contract(rows_grad, down_mat, 1, 1)
    sigmoid = jax.nn.sigmoid(gate_proj)
    active = gate_proj * sigmoid
    hidden = (active * up_proj).astype(jnp.bfloat16)
    d_gate = (back_grad * up_proj * sigmoid * (1.0 + gate_proj * (1.0 - sigmoid))).astype(
        jnp.bfloat16
    )
    d_upper = (back_grad * active).astype(jnp.bfloat16)
    input_grad = contract(d_gate, gate_mat, 1, 1) + contract(d_upper, up_mat, 1, 1)
    return (input_grad.astype(jnp.bfloat16), hidden, d_gate, d_upper)


def mirror_swaps(tok_rows):
    for bit_index in range(lax.axis_size("section").bit_length() - 1):
        tok_rows = swapped(tok_rows, "section", bit_index)
    return tok_rows


def body(saved_rows, grad_out, expert_ids, combine, w_gate, w_up, w_down):
    tok_rows = saved_rows[0]
    tok_rows = mirror_swaps(tok_rows)
    model_width = tok_rows.shape[1]
    sources = lax.axis_size("expert")
    shares = sources // EXPERTS
    chosen = expert_ids[0, :, 0]
    weights = combine[0, :, 0]
    choose = (chosen[:, None] == jnp.arange(EXPERTS, dtype=jnp.int32)[None, :]).astype(jnp.int32)
    before = jnp.cumsum(choose, axis=0) - choose
    slot_of = jnp.sum(before * choose, axis=1)
    target = chosen * CAP + slot_of
    placing = (jnp.arange(EXPERTS * CAP, dtype=jnp.int32)[:, None] == target[None, :]).astype(
        jnp.bfloat16
    )
    counts = jnp.sum(choose, axis=0)
    scaled = (weights[:, None] * grad_out[0].astype(jnp.float32)).astype(jnp.bfloat16)
    packed_in = jnp.dot(placing, tok_rows, preferred_element_type=jnp.float32).astype(jnp.bfloat16)
    packed_grad = jnp.dot(placing, scaled, preferred_element_type=jnp.float32).astype(jnp.bfloat16)

    def copies(packed):
        grid_view = packed.reshape(EXPERTS, 1, CAP, model_width)
        return jnp.broadcast_to(grid_view, (EXPERTS, shares, CAP, model_width)).reshape(
            sources, CAP, model_width
        )

    send_counts = jnp.broadcast_to(counts[:, None], (EXPERTS, shares)).reshape(sources)
    got_in, got_grad, got_counts = (
        lax.all_to_all(copies(packed_in), "expert", split_axis=0, concat_axis=0, tiled=True),
        lax.all_to_all(copies(packed_grad), "expert", split_axis=0, concat_axis=0, tiled=True),
        lax.all_to_all(send_counts, "expert", split_axis=0, concat_axis=0, tiled=True),
    )
    full_gate, full_up, full_down = (
        lax.all_gather(w_gate, "dp", axis=1, tiled=True),
        lax.all_gather(w_up, "dp", axis=1, tiled=True),
        lax.all_gather(w_down, "dp", axis=2, tiled=True),
    )
    gate_mat = full_gate[0]
    up_mat = full_up[0]
    down_mat = full_down[0]
    hidden_units = gate_mat.shape[1]
    slot_total = sources * CAP
    padded_len = -(-slot_total // block_rows) * block_rows
    zero_rows = jnp.zeros((padded_len - slot_total, model_width), jnp.bfloat16)
    flat_in = jnp.concatenate([got_in.reshape(slot_total, model_width), zero_rows], axis=0)
    flat_grad = jnp.concatenate([got_grad.reshape(slot_total, model_width), zero_rows], axis=0)
    start_carry = (
        jnp.zeros((padded_len, model_width), jnp.bfloat16),
        jnp.zeros((padded_len, hidden_units), jnp.bfloat16),
        jnp.zeros((padded_len, hidden_units), jnp.bfloat16),
        jnp.zeros((padded_len, hidden_units), jnp.bfloat16),
    )

    def add_block(carry_all, rows_in, rows_grad, row_start):
        results = rows_backward(rows_in, rows_grad, gate_mat, up_mat, down_mat)
        return tuple(
            (
                lax.dynamic_update_slice_in_dim(held, fresh, row_start, 0)
                for held, fresh in zip(carry_all, results)
            )
        )

    offsets = jnp.cumsum(got_counts) - got_counts
    live_total = jnp.sum(got_counts)
    positions = jnp.arange(padded_len, dtype=jnp.int32)
    source_ids = jnp.arange(sources, dtype=jnp.int32)
    owner_src = jnp.sum((positions[:, None] >= offsets[None, :]).astype(jnp.int32), axis=1) - 1
    owner_hit = (owner_src[:, None] == source_ids[None, :]).astype(jnp.int32)
    within = positions - jnp.sum(owner_hit * offsets[None, :], axis=1)
    is_valid = positions < live_total
    pick_rows = jnp.where(is_valid, owner_src * CAP + within, 0)

    def live_block(block_no, carry_all):
        row_start = block_no * block_rows
        chosen_rows = lax.dynamic_slice_in_dim(pick_rows, row_start, block_rows)
        keep_rows = lax.dynamic_slice_in_dim(is_valid, row_start, block_rows)[:, None]
        rows_in = jnp.where(
            keep_rows, jnp.take(flat_in, chosen_rows, axis=0), jnp.zeros((), jnp.bfloat16)
        )
        rows_grad = jnp.where(
            keep_rows, jnp.take(flat_grad, chosen_rows, axis=0), jnp.zeros((), jnp.bfloat16)
        )
        return add_block(carry_all, rows_in, rows_grad, row_start)

    count_blocks = (live_total + block_rows - 1) // block_rows
    grad_rows, hidden_rows, gate_rows, upper_rows = lax.fori_loop(
        0, count_blocks, live_block, start_carry
    )
    slot_ids = jnp.arange(slot_total, dtype=jnp.int32)
    slot_hit = ((slot_ids // CAP)[:, None] == source_ids[None, :]).astype(jnp.int32)
    slot_base = jnp.sum(slot_hit * offsets[None, :], axis=1)
    slot_count = jnp.sum(slot_hit * got_counts[None, :], axis=1)
    slot_pos = slot_ids % CAP
    is_alive = (slot_pos < slot_count)[:, None]
    fetch_index = jnp.where(slot_pos < slot_count, slot_base + slot_pos, 0)
    nothing = jnp.zeros((), jnp.bfloat16)
    slot_grads = jnp.where(is_alive, jnp.take(grad_rows, fetch_index, axis=0), nothing)
    hidden_slot = jnp.where(is_alive, jnp.take(hidden_rows, fetch_index, axis=0), nothing)
    gate_slot = jnp.where(is_alive, jnp.take(gate_rows, fetch_index, axis=0), nothing)
    upper_slot = jnp.where(is_alive, jnp.take(upper_rows, fetch_index, axis=0), nothing)
    sum_gate = contract(flat_in, gate_slot, 0, 0)
    sum_up = contract(flat_in, upper_slot, 0, 0)
    sum_down = contract(hidden_slot, flat_grad, 0, 0)
    returned = lax.all_to_all(
        slot_grads.reshape(sources, CAP, model_width),
        "expert",
        split_axis=0,
        concat_axis=0,
        tiled=True,
    )
    merged = jnp.sum(
        returned.reshape(EXPERTS, shares, CAP, model_width).astype(jnp.float32), axis=1
    )
    merged = merged.reshape(EXPERTS * CAP, model_width).astype(jnp.bfloat16)
    grad_in = contract(placing, merged, 0, 0).astype(jnp.bfloat16)
    grad_gate, grad_up, grad_down = (
        lax.psum_scatter(
            sum_gate.astype(jnp.bfloat16), "dp", scatter_dimension=0, tiled=True
        ).astype(jnp.float32),
        lax.psum_scatter(sum_up.astype(jnp.bfloat16), "dp", scatter_dimension=0, tiled=True).astype(
            jnp.float32
        ),
        lax.psum_scatter(
            sum_down.astype(jnp.bfloat16), "dp", scatter_dimension=1, tiled=True
        ).astype(jnp.float32),
    )
    return (
        grad_in[None],
        grad_gate.astype(jnp.bfloat16)[None],
        grad_up.astype(jnp.bfloat16)[None],
        grad_down.astype(jnp.bfloat16)[None],
    )


def solution(mesh):
    return jax.shard_map(
        body,
        mesh=mesh,
        in_specs=(
            P("section", ("expert", "dp"), None),
            P("section", ("expert", "dp"), None),
            P("section", ("expert", "dp"), None),
            P("section", ("expert", "dp"), None),
            P("section", "dp", "expert"),
            P("section", "dp", "expert"),
            P("section", "expert", "dp"),
        ),
        out_specs=(
            P("section", ("expert", "dp"), None),
            P("section", "dp", "expert"),
            P("section", "dp", "expert"),
            P("section", "expert", "dp"),
        ),
        check_vma=False,
    )
```

profile of v0, /device:TPU:30, one launch (start us, length us, event | category | flops | bytes accessed | tf_op | source)
XLA Modules:
  0.0 689.3 jit_solution(16232288779926015356)
XLA Ops:
  9.7 11.4 %all-to-all-start = ((s32[16,1,1]{2,1,0:T(1,128)}), s32[16,1,1]{2,1,0:T(1,128)S(1)}, u32[]{:S(2)}, u32[]{:S(2)}) async-start(s32[16,1,1]{2,1,0:T(1,128)} %all_to_all.20), calls=%async_computation | async-start | bytes 16384 | tf_op jit(solution)/shard_map/all_to_all | solution.py:77
  31.6 7.5 %all-to-all-start.1 = ((bf16[16,48,4096]{2,1,0:T(8,128)(2,1)}), bf16[16,48,4096]{2,1,0:T(8,128)(2,1)}, u32[]{:S(2)}, u32[]{:S(2)}) async-start(bf16[16,48,4096]{2,1,0:T(8,128)(2,1)} %bitcast.59), calls=%async_computation.1 | async-start | bytes 12582912 | tf_op jit(solution)/shard_map/all_to_all | solution.py:76
  39.9 48.0 %collective-permute-done = bf16[128,4096]{1,0:T(8,128)(2,1)S(1)} collective-permute-done((bf16[128,4096]{1,0:T(8,128)(2,1)S(1)}, bf16[128,4096]{1,0:T(8,128)(2,1)S(1)}, u32[]{:S(2)}, u32[]{:S(2)}) %collective-permute-start) | collective-permute-done | bytes 1048608 | tf_op jit(solution)/shard_map/ppermute | solution.py:14
  88.8 23.1 %collective-permute-done.1 = bf16[128,4096]{1,0:T(8,128)(2,1)S(1)} collective-permute-done((bf16[128,4096]{1,0:T(8,128)(2,1)S(1)}, bf16[128,4096]{1,0:T(8,128)(2,1)S(1)}, u32[]{:S(2)}, u32[]{:S(2)}) %collective-permute-start.1) | collective-permute-done | bytes 1048608 | tf_op jit(solution)/shard_map/ppermute | solution.py:14
  112.6 22.6 %collective-permute-done.2 = bf16[128,4096]{1,0:T(8,128)(2,1)S(1)} collective-permute-done((bf16[128,4096]{1,0:T(8,128)(2,1)S(1)}, bf16[128,4096]{1,0:T(8,128)(2,1)S(1)}, u32[]{:S(2)}, u32[]{:S(2)}) %collective-permute-start.2) | collective-permute-done | bytes 1048608 | tf_op jit(solution)/shard_map/ppermute | solution.py:14
  135.7 41.0 %all-to-all-done.1 = bf16[16,48,4096]{2,1,0:T(8,128)(2,1)} async-done(((bf16[16,48,4096]{2,1,0:T(8,128)(2,1)}), bf16[16,48,4096]{2,1,0:T(8,128)(2,1)}, u32[]{:S(2)}, u32[]{:S(2)}) %all-to-all-start.1) | async-done | bytes 6291488 | tf_op jit(solution)/shard_map/all_to_all | solution.py:76
  180.1 13.2 %all-to-all-start.2 = ((bf16[16,48,4096]{2,1,0:T(8,128)(2,1)}), bf16[16,48,4096]{2,1,0:T(8,128)(2,1)}, u32[]{:S(2)}, u32[]{:S(2)}) async-start(bf16[16,48,4096]{2,1,0:T(8,128)(2,1)} %bitcast.58), calls=%async_computation.2 | async-start | bytes 12582912 | tf_op jit(solution)/shard_map/all_to_all | solution.py:75
  199.0 15.3 %all-gather.6.cloned.1.call-done = bf16[1,4096,384]{2,1,0:T(8,128)(2,1)} async-done(((bf16[1,2048,384]{2,1,0:T(8,128)(2,1)}), bf16[1,4096,384]{2,1,0:T(8,128)(2,1)}) %all-gather.6.cloned.1.call-update) | async-done | bytes 3145744 | tf_op jit(solution)/shard_map/all_gather | solution.py:81
  214.3 20.6 %all-gather.8.cloned.1.call-done = bf16[1,4096,384]{2,1,0:T(8,128)(2,1)} async-done(((bf16[1,2048,384]{2,1,0:T(8,128)(2,1)}), bf16[1,4096,384]{2,1,0:T(8,128)(2,1)}) %all-gather.8.cloned.1.call-update) | async-done | bytes 3145744 | tf_op jit(solution)/shard_map/all_gather | solution.py:80
  234.9 20.6 %all-gather.4.cloned.1.call-done = bf16[1,384,4096]{2,1,0:T(8,128)(2,1)} async-done(((bf16[1,384,2048]{2,1,0:T(8,128)(2,1)}), bf16[1,384,4096]{2,1,0:T(8,128)(2,1)}) %all-gather.4.cloned.1.call-update) | async-done | bytes 3145744 | tf_op jit(solution)/shard_map/all_gather | solution.py:82
  255.5 76.9 %all-to-all-done.2 = bf16[16,48,4096]{2,1,0:T(8,128)(2,1)} async-done(((bf16[16,48,4096]{2,1,0:T(8,128)(2,1)}), bf16[16,48,4096]{2,1,0:T(8,128)(2,1)}, u32[]{:S(2)}, u32[]{:S(2)}) %all-to-all-start.2) | async-done | bytes 6291488 | tf_op jit(solution)/shard_map/all_to_all | solution.py:75
  338.4 144.0 %while.16 = (s32[]{:T(128)}, bf16[768,4096]{1,0:T(8,128)(2,1)}, bf16[768,384]{1,0:T(8,128)(2,1)}, bf16[768,384]{1,0:T(8,128)(2,1)}, bf16[768,384]{1,0:T(8,128)(2...) while((s32[]{:T(128)}, bf16[768,4096]{1,0:T(8,128)(2,1)}, ...), condition=%wide.region_10.12_spmd, body=%wide.region_9.11_spmd.sunk | while | flops 2018199296 | bytes 46571412 | solution.py:132
  338.4 6.8 gather_fusion.1
  347.3 6.8 gather_fusion
  362.5 6.8 gather_fusion.1
  443.3 6.8 gather_fusion
  467.2 6.8 gather_fusion
  485.9 8.1 %convolution_convert_fusion.2 = bf16[4096,384]{1,0:T(8,128)(2,1)} fusion(bf16[768,4096]{1,0:T(8,128)(2,1)} %bitcast.11, bf16[768,384]{1,0:T(8,128)(2,1)S(1)} %gather_fusion.3, pred[768]{0:T(1024)(128)(4,1)S(1)} %get-tuple-element.120, pred[768]{0:T(1024)(128)(4,1)S(1)} %get-tuple-element.122), kind=kOutput, calls=%fused_computation.35 | convolution fusion | flops 2418081792 | bytes 10028544 | tf_op jit(solution)/shard_map/dot_general | solution.py:18
  497.8 8.1 %convolution_convert_fusion.1 = bf16[4096,384]{1,0:T(8,128)(2,1)} fusion(bf16[768,4096]{1,0:T(8,128)(2,1)} %bitcast.11, bf16[768,384]{1,0:T(8,128)(2,1)S(1)} %gather_fusion.4, pred[768]{0:T(1024)(128)(4,1)S(1)} %get-tuple-element.120, pred[768]{0:T(1024)(128)(4,1)S(1)} %get-tuple-element.122), kind=kOutput, calls=%fused_computation.34 | convolution fusion | flops 2418081792 | bytes 10028544 | tf_op jit(solution)/shard_map/dot_general | solution.py:18
  505.9 16.4 %gather_fusion.2 = bf16[768,4096]{1,0:T(8,128)(2,1)} fusion(bf16[768,4096]{1,0:T(8,128)(2,1)} %get-tuple-element.77, s32[1024]{0:T(1024)S(1)} %pad_clamp_fusion.2), kind=kCustom, calls=%fused_computation.5 | custom fusion | bytes 12585984 | tf_op jit(solution)/shard_map/jit(_take)/gather | solution.py:143
  522.3 6.9 %select_select_fusion.5 = bf16[16,48,4096]{2,1,0:T(8,128)(2,1)} fusion(bf16[16,48,4096]{2,1,0:T(8,128)(2,1)} %bitcast.57, pred[16,48]{1,0:T(8,128)(4,1)S(1)} %get-tuple-element.123, pred[16,48]{1,0:T(8,128)(4,1)S(1)} %get-tuple-element.124), kind=kLoop, calls=%fused_computation.32 | loop fusion | flops 6291456 | bytes 12584448 | tf_op jit(solution)/shard_map/jit(_where)/select_n | solution.py:143
  529.2 9.5 %all-to-all-start.3 = ((bf16[16,48,4096]{2,1,0:T(8,128)(2,1)}), bf16[16,48,4096]{2,1,0:T(8,128)(2,1)}, u32[]{:S(2)}, u32[]{:S(2)}) async-start(bf16[16,48,4096]{2,1,0:T(8,128)(2,1)} %select_select_fusion.5), calls=%async_computation.3 | async-start | bytes 12582912 | tf_op jit(solution)/shard_map/all_to_all | solution.py:150
  541.7 7.3 %convolution_convert_fusion = bf16[384,4096]{1,0:T(8,128)(2,1)} fusion(bf16[768,4096]{1,0:T(8,128)(2,1)} %bitcast.6, bf16[768,384]{1,0:T(8,128)(2,1)S(1)} %gather_fusion.5, pred[768]{0:T(1024)(128)(4,1)S(1)} %get-tuple-element.120, pred[768]{0:T(1024)(128)(4,1)S(1)} %get-tuple-element.122), kind=kOutput, calls=%fused_computation.33 | convolution fusion | flops 2418081792 | bytes 10028544 | tf_op jit(solution)/shard_map/dot_general | solution.py:18
  549.0 127.9 %all-to-all-done.3 = bf16[16,48,4096]{2,1,0:T(8,128)(2,1)} async-done(((bf16[16,48,4096]{2,1,0:T(8,128)(2,1)}), bf16[16,48,4096]{2,1,0:T(8,128)(2,1)}, u32[]{:S(2)}, u32[]{:S(2)}) %all-to-all-start.3) | async-done | bytes 6291488 | tf_op jit(solution)/shard_map/all_to_all | solution.py:150
  (142 shorter events, 155.9 us)
Async XLA Ops:
  9.7 18.5 %all-to-all-start = ((s32[16,1,1]{2,1,0:T(1,128)}), s32[16,1,1]{2,1,0:T(1,128)S(1)}, u32[]{:S(2)}, u32[]{:S(2)}) async-start(s32[16,1,1]{2,1,0:T(1,128)} %all_to_all.20), calls=%async_computation | async-start | bytes 16384 | tf_op jit(solution)/shard_map/all_to_all | solution.py:77
  31.6 7.5 %copy-start.5 = (bf16[1,128,4096]{2,1,0:T(8,128)(2,1)S(1)}, bf16[1,128,4096]{2,1,0:T(8,128)(2,1)}, u32[]{:S(2)}) copy-start(bf16[1,128,4096]{2,1,0:T(8,128)(2,1)} %param.13) | copy-start | bytes 3145732
  31.6 145.1 %all-to-all-start.1 = ((bf16[16,48,4096]{2,1,0:T(8,128)(2,1)}), bf16[16,48,4096]{2,1,0:T(8,128)(2,1)}, u32[]{:S(2)}, u32[]{:S(2)}) async-start(bf16[16,48,4096]{2,1,0:T(8,128)(2,1)} %bitcast.59), calls=%async_computation.1 | async-start | bytes 12582912 | tf_op jit(solution)/shard_map/all_to_all | solution.py:76
  39.1 48.8 %collective-permute-start = (bf16[128,4096]{1,0:T(8,128)(2,1)S(1)}, bf16[128,4096]{1,0:T(8,128)(2,1)S(1)}, u32[]{:S(2)}, u32[]{:S(2)}) collective-permute-start(bf16[128,4096]{1,0:T(8,128)(2,1)S(1)} %bitcast.71), channel_id=1, source_target_pairs={{0,32},{32,0},{64,96},{96,64},{128,160},{160,128},{192,224},{224,1... | collective-permute-start | bytes 3145736 | tf_op jit(solution)/shard_map/ppermute | solution.py:14
  87.9 23.9 %collective-permute-start.1 = (bf16[128,4096]{1,0:T(8,128)(2,1)S(1)}, bf16[128,4096]{1,0:T(8,128)(2,1)S(1)}, u32[]{:S(2)}, u32[]{:S(2)}) collective-permute-start(bf16[128,4096]{1,0:T(8,128)(2,1)S(1)} %collective-permute-done), channel_id=1, source_target_pairs={{0,64},{32,96},{64,0},{96,32},{128,192},{160,224},{192,128},{224,1... | collective-permute-start | bytes 3145736 | tf_op jit(solution)/shard_map/ppermute | solution.py:14
  111.8 23.3 %collective-permute-start.2 = (bf16[128,4096]{1,0:T(8,128)(2,1)S(1)}, bf16[128,4096]{1,0:T(8,128)(2,1)S(1)}, u32[]{:S(2)}, u32[]{:S(2)}) collective-permute-start(bf16[128,4096]{1,0:T(8,128)(2,1)S(1)} %collective-permute-done.1), channel_id=1, source_target_pairs={{0,128},{32,160},{64,192},{96,224},{128,0},{160,32},{192,64},{224,... | collective-permute-start | bytes 3145736 | tf_op jit(solution)/shard_map/ppermute | solution.py:14
  180.1 152.2 %all-to-all-start.2 = ((bf16[16,48,4096]{2,1,0:T(8,128)(2,1)}), bf16[16,48,4096]{2,1,0:T(8,128)(2,1)}, u32[]{:S(2)}, u32[]{:S(2)}) async-start(bf16[16,48,4096]{2,1,0:T(8,128)(2,1)} %bitcast.58), calls=%async_computation.2 | async-start | bytes 12582912 | tf_op jit(solution)/shard_map/all_to_all | solution.py:75
  193.4 20.9 %all-gather.6.cloned.1.call-start = ((), (), s32[]{:S(2)}) async-start(), calls=%async_computation.8 | async-start | bytes 4718592 | tf_op jit(solution)/shard_map/all_gather | solution.py:81
  194.1 40.8 %all-gather.8.cloned.1.call-start = ((), (), s32[]{:S(2)}) async-start(), calls=%async_computation.9 | async-start | bytes 4718592 | tf_op jit(solution)/shard_map/all_gather | solution.py:80
  194.8 60.6 %all-gather.4.cloned.1.call-start = ((), (), s32[]{:S(2)}) async-start(), calls=%async_computation.7 | async-start | bytes 4718592 | tf_op jit(solution)/shard_map/all_gather | solution.py:82
  195.6 486.9 %reduce-scatter.4.cloned.1.call-start = ((), (), s32[]{:S(2)}) async-start(), calls=%async_computation.10 | async-start | bytes 4718592 | tf_op jit(solution)/shard_map/reduce_scatter | solution.py:163
  332.4 6.0 copy-start
  354.1 3.4 copy-start.1
  354.1 3.4 copy-start.4
  378.1 3.4 copy-start.1
  378.1 3.4 copy-start.4
  402.1 3.4 copy-start.4
  426.0 3.4 copy-start.4
  450.0 3.4 copy-start.4
  474.0 3.4 copy-start.4
  494.1 188.4 %reduce-scatter.6.cloned.1.call-start = ((), (), s32[]{:S(2)}) async-start(), calls=%async_computation.11 | async-start | bytes 4718592 | tf_op jit(solution)/shard_map/reduce_scatter | solution.py:166
  529.2 9.8 %copy-start.2 = (bf16[768,384]{1,0:T(8,128)(2,1)S(1)}, bf16[768,384]{1,0:T(8,128)(2,1)}, u32[]{:S(2)}) copy-start(bf16[768,384]{1,0:T(8,128)(2,1)} %get-tuple-element.80) | copy-start | bytes 1769476
  529.2 147.6 %all-to-all-start.3 = ((bf16[16,48,4096]{2,1,0:T(8,128)(2,1)}), bf16[16,48,4096]{2,1,0:T(8,128)(2,1)}, u32[]{:S(2)}, u32[]{:S(2)}) async-start(bf16[16,48,4096]{2,1,0:T(8,128)(2,1)} %select_select_fusion.5), calls=%async_computation.3 | async-start | bytes 12582912 | tf_op jit(solution)/shard_map/all_to_all | solution.py:150
  538.7 143.7 %reduce-scatter.8.cloned.1.call-start = ((), (), s32[]{:S(2)}) async-start(), calls=%async_computation.12 | async-start | bytes 4718592 | tf_op jit(solution)/shard_map/reduce_scatter | solution.py:169
  (5 other events, 14.8 us)
Sparse Core Ops, SparseCore 0:
  196.0 18.2 all-gather.5
  216.1 18.7 all-gather.7
  236.7 18.7 all-gather.3
  494.2 17.1 reduce-scatter.3
  514.5 17.4 reduce-scatter.5
  549.1 16.9 reduce-scatter.7
where the time goes:
time: 693 us; the launch traced here: 689 us
  waiting for transfers between devices  403 us (58%)
  local copies, waits for them, and re-layouts  121 us (17%)
  matrix products  89 us (13%)
  starting transfers between devices  44.6 us (6%)
  other arithmetic  16.6 us (2%)
  between operations  14.9 us (2%)
    all_to_all x1, waiting for transfers between devices, body(): lax.all_to_all(slot_grads.reshape(sources, CAP, model_width), 'expert', s...  128 us
    ppermute x3, waiting for transfers between devices, swapped(): lax.ppermute(x, axis, [(i, i ^ 1 << stride) for i in range(lax.axis_size(...  93.7 us
    all_to_all x1, waiting for transfers between devices, body(): lax.all_to_all(copies(packed_in), 'expert', split_axis=0, concat_axis=0,...  76.9 us
    dot_general x22, matrix products, contract(): lax.dot_general(left_mat, right_mat, (((left_dim,), (right_dim,)), ((), (...  65.1 us
    all_to_all x1, waiting for transfers between devices, body(): lax.all_to_all(copies(packed_grad), 'expert', split_axis=0, concat_axis=0...  41 us
    gather x6, local copies, waits for them, and re-layouts, live_block(): jnp.take(flat_grad, chosen_rows, axis=0)  40.6 us
    gather x6, local copies, waits for them, and re-layouts, live_block(): jnp.take(flat_in, chosen_rows, axis=0)  40.6 us
    all_gather x1, waiting for transfers between devices, body(): lax.all_gather(w_down, 'dp', axis=2, tiled=True)  20.6 us
  transfers between devices with their start and end apart: 13, of which 10 were waited for; matrix products, arithmetic and copies ran while one was open for 8% of the time, Pallas kernels for 0%

commit v1 on v0

v1 whole, which is shorter than its diff:
```python
import functools

import jax
import jax.numpy as jnp
from jax import lax
from jax.experimental import pallas as pl
from jax.experimental.pallas import tpu as pltpu
from jax.sharding import PartitionSpec as P

EXPERTS = 4
CAP = 48
SHARES = 4
RING = 8
STEPS = 9
COLS = 256
MESH = pl.DeviceIdType.MESH
F32 = jnp.float32
BF16 = jnp.bfloat16


def dot(a, b, dim_a, dim_b):
    return lax.dot_general(a, b, (((dim_a,), (dim_b,)), ((), ())), preferred_element_type=F32)


def kernel(
    px, pz, wg, wu, wd,
    f_out, gg_out, gu_out, gd_out,
    xb, zb, wgu, wdn, pb, rb, d2, hd, g1, g2,
    rx, ent_send, fwd_send, rr, rsend, fr, wrecv, wsend, wloc, grecv, gsend, gloc,
):
    sec, k, rep = lax.axis_index("section"), lax.axis_index("expert"), lax.axis_index("dp")
    mirror = lax.axis_size("section") - 1 - sec
    yh, z = k // RING, k % RING
    seg, c = z // SHARES, z % SHARES
    mine = 2 * yh + seg
    other = 1 - rep
    width = xb.shape[-1]
    half = width // 2
    units = hd.shape[-1]

    def zof(pos):
        return (SHARES * seg + pos + RING) % RING

    def here(expert):
        return (sec, expert, rep)

    twin = (sec, k, other)

    def remote(src, dst, send, recv, dev):
        return pltpu.make_async_remote_copy(
            src_ref=src, dst_ref=dst, send_sem=send, recv_sem=recv, device_id=dev, device_id_type=MESH
        )

    def entry(e, t):
        ye, te = e // 2, e % 2
        far = jnp.where(c < 2, SHARES - 1, 0)
        z_in = jnp.where(seg == te, z, te * SHARES + far)
        src, buf, s = ((px, xb, mirror), (pz, zb, sec))[t]
        return remote(
            src.at[e], buf.at[z, yh], ent_send.at[t, e], rx.at[t, z], (s, ye * RING + z_in, rep)
        )

    own_copy = [
        pltpu.make_async_copy(pz.at[e], zb.at[z, yh], rx.at[1, z]) for e in range(EXPERTS)
    ]
    for e in range(EXPERTS):
        @pl.when(mine == e)
        def _():
            own_copy[e].start()

        @pl.when(mine != e)
        def _():
            entry(e, 1).start()
    for e in range(EXPERTS):
        entry(e, 0).start()

    rows = pl.ds(pl.multiple_of(rep * half, half), half)
    rows_far = pl.ds(pl.multiple_of(other * half, half), half)
    w_parts = (
        (wg, lambda r: wgu.at[r, pl.ds(0, units)]),
        (wu, lambda r: wgu.at[r, pl.ds(units, units)]),
        (wd, lambda r: wdn.at[:, r]),
    )
    for i, (src, dst) in enumerate(w_parts):
        pltpu.make_async_copy(src, dst(rows), wloc.at[i]).start()
        remote(src, dst(rows), wsend.at[i], wrecv.at[i], twin).start()

    right, left = here(k + 1), here(k - 1)

    def forward(t, buf, side, zz):
        return remote(
            buf.at[zz], buf.at[zz], fwd_send.at[t, side, zz], rx.at[t, zz], (left, right)[side]
        )

    def arrive(pos, go_left, go_right):
        zz = zof(pos)
        for t, buf in ((1, zb), (0, xb)):
            remote(
                buf.at[zz], buf.at[zz], fwd_send.at[t, 0, zz], rx.at[t, zz], twin
            ).wait_recv()
            for side, go in ((1, go_right), (0, go_left)):
                if go is not None:
                    @pl.when(go)
                    def _():
                        forward(t, buf, side, zz).start()

    def compute(zz):
        n_rows = 2 * CAP
        x = xb[zz].reshape(n_rows, width)
        gu = dot(x, wgu[...], 1, 0)
        back = dot(zb[zz].reshape(n_rows, width), wdn[...], 1, 1)
        gate, up = gu[:, :units], gu[:, units:]
        sig = jax.nn.sigmoid(gate)
        act = gate * sig
        hd[zz] = (act * up).astype(BF16)
        d_gate = (back * up * sig * (1.0 + gate * (1.0 - sig))).astype(BF16)
        d_up = (back * act).astype(BF16)
        d2[zz, :, :units] = d_gate
        d2[zz, :, units:] = d_up
        d = jnp.concatenate([d_gate, d_up], axis=1)
        chunk = 1024

        def part(n, _):
            cols = pl.ds(pl.multiple_of(n * chunk, chunk), chunk)
            pb[zz, :, :, cols] = dot(d, wgu[cols, :], 1, 1).astype(BF16).reshape(2, CAP, chunk)

        lax.fori_loop(0, width // chunk, part, None)

    def go_back(src, zz, side, at_end):
        slot = jnp.where(at_end, RING, zz) if side else zz
        return remote(
            src.at[zz], rb.at[slot], rsend.at[0, zz], rr.at[slot], (left, right)[side]
        )

    def go_home(src, zz, y):
        return remote(
            src.at[zz, y], f_out.at[mine], rsend.at[y, zz], fr.at[mine], here(y * RING + zz)
        )

    def add_part(zz):
        for y in range(2):
            rb[zz, y] = (rb[zz, y].astype(F32) + pb[zz, y].astype(F32)).astype(BF16)

    def wait_back(slot):
        remote(rb.at[slot], rb.at[slot], rsend.at[0, 0], rr.at[slot], twin).wait_recv()

    def step_conditions(j):
        in_left = (j >= 1) & (j <= c + 2)
        in_right = (j >= 1) & (j <= 5 - c)
        p_from_right = 6 - c - j
        p_from_left = j - c
        from_right = (c < 3) & (p_from_right >= -2) & (p_from_right <= c)
        from_left = (c > 0) & (p_from_left >= c) & (p_from_left <= 5)
        finish = j == jnp.where((c == 0) | (c == 3), 6, 4)
        return in_left, in_right, p_from_right, p_from_left, from_right, from_left, finish

    def home_copy():
        return pltpu.make_async_copy(pb.at[z, yh], f_out.at[mine], fr.at[mine])

    def weight_cols(m):
        return pl.ds(pl.multiple_of(m * COLS, COLS), COLS)

    n_all = RING * 2 * CAP

    def grads_in(m, _):
        cols = weight_cols(m)
        xt = xb[:, :, :, cols].reshape(n_all, COLS)
        wgu[cols, :] = dot(xt, d2[...].reshape(n_all, 2 * units), 0, 0).astype(BF16)

    def grads_down(m, _):
        cols = weight_cols(m)
        zt = zb[:, :, :, cols].reshape(n_all, COLS)
        wdn[:, cols] = dot(hd[...].reshape(n_all, units), zt, 0, 0).astype(BF16)

    per_half = half // COLS
    send_in = remote(wgu.at[rows_far], g1, gsend.at[0], grecv.at[0], twin)
    send_down = remote(wdn.at[:, rows_far], g2, gsend.at[1], grecv.at[1], twin)

    def step(j, _):
        in_left, in_right, p_r, p_l, from_right, from_left, finish = step_conditions(j)

        @pl.when(j == 0)
        def _():
            arrive(c, c > 0, c < 3)

        @pl.when(in_left)
        def _():
            arrive(c - j, None, c < 3)

        @pl.when(in_right)
        def _():
            arrive(c + j, c > 0, None)

        @pl.when(j == 0)
        def _():
            for i, (src, dst) in enumerate(w_parts):
                pltpu.make_async_copy(src, dst(rows), wloc.at[i]).wait()
                remote(src, dst(rows_far), wsend.at[i], wrecv.at[i], twin).wait_recv()

        def side_step(side, _):
            pos = jnp.where(side == 0, c - j, c + j)
            valid = jnp.where(side == 0, (j == 0) | in_left, in_right)

            @pl.when(valid)
            def _():
                zz = zof(pos)
                compute(zz)

                @pl.when((j > 0) & (side == 0) & (c == 3))
                def _():
                    go_back(pb, zz, 0, False).start()

                @pl.when((side == 1) & (c == 0))
                def _():
                    go_back(pb, zz, 1, pos == 1).start()

        lax.fori_loop(0, 2, side_step, None)

        @pl.when(from_right)
        def _():
            zz = zof(p_r)
            wait_back(zz)

            @pl.when(p_r < c)
            def _():
                add_part(zz)

                @pl.when(c > 0)
                def _():
                    go_back(rb, zz, 0, False).start()

                @pl.when(c == 0)
                def _():
                    for y in range(2):
                        go_home(rb, zz, y).start()

        @pl.when(from_left)
        def _():
            zz = zof(p_l)

            @pl.when(p_l == c)
            def _():
                wait_back(RING)

            @pl.when(p_l > c)
            def _():
                wait_back(zz)
                add_part(zz)

                @pl.when(c < 3)
                def _():
                    go_back(rb, zz, 1, p_l == c + 1).start()

                @pl.when(c == 3)
                def _():
                    for y in range(2):
                        go_home(rb, zz, y).start()

        @pl.when(finish)
        def _():
            for y in range(2):
                @pl.when(c == 0)
                def _():
                    pb[z, y] = (pb[z, y].astype(F32) + rb[z, y].astype(F32)).astype(BF16)

                @pl.when(c == 3)
                def _():
                    pb[z, y] = (pb[z, y].astype(F32) + rb[RING, y].astype(F32)).astype(BF16)

                @pl.when((c > 0) & (c < 3))
                def _():
                    total = pb[z, y].astype(F32) + rb[z, y].astype(F32)
                    pb[z, y] = (total + rb[RING, y].astype(F32)).astype(BF16)

            home_copy().start()
            go_home(pb, z, 1 - yh).start()

        @pl.when(j == 5)
        def _():
            lax.fori_loop(other * per_half, (other + 1) * per_half, grads_in, None)
            send_in.start()

        @pl.when(j == 6)
        def _():
            lax.fori_loop(other * per_half, (other + 1) * per_half, grads_down, None)
            send_down.start()
            lax.fori_loop(rep * per_half, (rep + 1) * per_half, grads_in, None)

        @pl.when(j == 7)
        def _():
            lax.fori_loop(rep * per_half, (rep + 1) * per_half, grads_down, None)

    lax.fori_loop(0, STEPS, step, None)

    piece = 512

    send_in.wait_recv()

    def add_in(m, _):
        at = pl.ds(pl.multiple_of(m * piece, piece), piece)
        own = wgu[pl.ds(pl.multiple_of(rep * half + m * piece, piece), piece), :]
        g1[at, :] = (g1[at, :].astype(F32) + own.astype(F32)).astype(BF16)

    lax.fori_loop(0, half // piece, add_in, None)
    outs = [
        pltpu.make_async_copy(g1.at[:, pl.ds(0, units)], gg_out, gloc.at[0]),
        pltpu.make_async_copy(g1.at[:, pl.ds(units, units)], gu_out, gloc.at[1]),
        pltpu.make_async_copy(g2, gd_out, gloc.at[2]),
    ]
    outs[0].start()
    outs[1].start()
    send_down.wait_recv()

    def add_down(m, _):
        at = pl.ds(pl.multiple_of(m * piece, piece), piece)
        own = wdn[:, pl.ds(pl.multiple_of(rep * half + m * piece, piece), piece)]
        g2[:, at] = (g2[:, at].astype(F32) + own.astype(F32)).astype(BF16)

    lax.fori_loop(0, half // piece, add_down, None)
    outs[2].start()

    for e in range(EXPERTS):
        remote(f_out.at[e], f_out.at[e], rsend.at[0, 0], fr.at[e], twin).wait_recv()

    for e in range(EXPERTS):
        entry(e, 0).wait_send()

        @pl.when(mine != e)
        def _():
            entry(e, 1).wait_send()
    for i, (src, dst) in enumerate(w_parts):
        remote(src, dst(rows), wsend.at[i], wrecv.at[i], twin).wait_send()
    send_in.wait_send()
    send_down.wait_send()

    def drain(j, _):
        in_left, in_right, p_r, p_l, from_right, from_left, finish = step_conditions(j)

        def forwarded(go, side, pos):
            @pl.when(go)
            def _():
                for t, buf in ((1, zb), (0, xb)):
                    forward(t, buf, side, zof(pos)).wait_send()

        forwarded(((j == 0) | in_left) & (c < 3), 1, c - j)
        forwarded(((j == 0) | in_right) & (c > 0), 0, c + j)

        @pl.when(in_left & (c == 3))
        def _():
            go_back(pb, zof(c - j), 0, False).wait_send()

        @pl.when(in_right & (c == 0))
        def _():
            go_back(pb, zof(c + j), 1, False).wait_send()

        @pl.when(from_right & (p_r < c) & (c > 0))
        def _():
            go_back(rb, zof(p_r), 0, False).wait_send()

        @pl.when(from_right & (p_r < c) & (c == 0))
        def _():
            for y in range(2):
                go_home(rb, zof(p_r), y).wait_send()

        @pl.when(from_left & (p_l > c) & (c < 3))
        def _():
            go_back(rb, zof(p_l), 1, False).wait_send()

        @pl.when(from_left & (p_l > c) & (c == 3))
        def _():
            for y in range(2):
                go_home(rb, zof(p_l), y).wait_send()

        @pl.when(finish)
        def _():
            go_home(pb, z, 1 - yh).wait_send()

    lax.fori_loop(0, STEPS, drain, None)
    for out in outs:
        out.wait()


def placing_of(chosen):
    n_tok = chosen.shape[0]
    choose = chosen[:, None] == jnp.arange(EXPERTS, dtype=jnp.int32)[None, :]
    tok = jnp.arange(n_tok, dtype=jnp.int32)
    lower = (tok[:, None] > tok[None, :]).astype(BF16)
    before = dot(lower, choose.astype(BF16), 1, 0)
    slot = jnp.sum(jnp.where(choose, before, 0.0), axis=1).astype(jnp.int32)
    target = chosen * CAP + slot
    return (jnp.arange(EXPERTS * CAP, dtype=jnp.int32)[:, None] == target[None, :]).astype(BF16)


def body(saved_rows, grad_out, expert_ids, combine, w_gate, w_up, w_down):
    n_sec = lax.axis_size("section")
    chosen = expert_ids[0, :, 0]
    chosen_far = lax.ppermute(chosen, "section", [(i, n_sec - 1 - i) for i in range(n_sec)])
    width = saved_rows.shape[2]
    units = w_gate.shape[2]
    placing = placing_of(chosen)
    scaled = (combine[0] * grad_out[0].astype(F32)).astype(BF16)
    pz = dot(placing, scaled, 1, 0).astype(BF16).reshape(EXPERTS, CAP, width)
    px = dot(placing_of(chosen_far), saved_rows[0], 1, 0).astype(BF16)
    px = px.reshape(EXPERTS, CAP, width)
    half = width // 2
    dma = pltpu.SemaphoreType.DMA
    outs = pl.pallas_call(
        kernel,
        out_shape=(
            jax.ShapeDtypeStruct((EXPERTS, CAP, width), BF16),
            jax.ShapeDtypeStruct((half, units), BF16),
            jax.ShapeDtypeStruct((half, units), BF16),
            jax.ShapeDtypeStruct((units, half), BF16),
        ),
        in_specs=[pl.BlockSpec(memory_space=pl.ANY)] * 5,
        out_specs=[pl.BlockSpec(memory_space=pl.ANY)] * 4,
        scratch_shapes=[
            pltpu.VMEM((RING, 2, CAP, width), BF16),
            pltpu.VMEM((RING, 2, CAP, width), BF16),
            pltpu.VMEM((width, 2 * units), BF16),
            pltpu.VMEM((units, width), BF16),
            pltpu.VMEM((RING, 2, CAP, width), BF16),
            pltpu.VMEM((RING + 1, 2, CAP, width), BF16),
            pltpu.VMEM((RING, 2 * CAP, 2 * units), BF16),
            pltpu.VMEM((RING, 2 * CAP, units), BF16),
            pltpu.VMEM((half, 2 * units), BF16),
            pltpu.VMEM((units, half), BF16),
            dma((2, RING)),
            dma((2, EXPERTS)),
            dma((2, 2, RING)),
            dma((RING + 1,)),
            dma((2, RING)),
            dma((EXPERTS,)),
            dma((3,)),
            dma((3,)),
            dma((3,)),
            dma((2,)),
            dma((2,)),
            dma((3,)),
        ],
        compiler_params=pltpu.CompilerParams(
            has_side_effects=True, vmem_limit_bytes=60 * 1024 * 1024
        ),
    )(px, pz, w_gate[0], w_up[0], w_down[0])
    merged, grad_gate, grad_up, grad_down = outs
    grad_in = dot(placing, merged.reshape(EXPERTS * CAP, width), 0, 0).astype(BF16)
    return grad_in[None], grad_gate[None], grad_up[None], grad_down[None]


def solution(mesh):
    return jax.shard_map(
        body,
        mesh=mesh,
        in_specs=(
            P("section", ("expert", "dp"), None),
            P("section", ("expert", "dp"), None),
            P("section", ("expert", "dp"), None),
            P("section", ("expert", "dp"), None),
            P("section", "dp", "expert"),
            P("section", "dp", "expert"),
            P("section", "expert", "dp"),
        ),
        out_specs=(
            P("section", ("expert", "dp"), None),
            P("section", "dp", "expert"),
            P("section", "dp", "expert"),
            P("section", "expert", "dp"),
        ),
        check_vma=False,
    )
```

time: 693 us -> 359 us (0.52)
  the two profiles are of different devices: /device:TPU:30 before, /device:TPU:50 now
where the time goes in v1:
time: 359 us; the launch traced here: 358 us
  Pallas kernels  341 us (95%)
  matrix products  8.73 us (2%)
  local copies, waits for them, and re-layouts  5.11 us (1%)
    pallas_call x1, Pallas kernels, body(): pl.pallas_call(kernel, out_shape=(jax.ShapeDtypeStruct((EXPERTS, CAP, wid...  341 us
    dot_general x5, matrix products, dot(): lax.dot_general(a, b, (((dim_a,), (dim_b,)), ((), ())), preferred_element...  8.73 us
  transfers between devices with their start and end apart: 1, of which 0 were waited for; matrix products, arithmetic and copies ran while one was open for 1% of the time, Pallas kernels for 0%

profile of v1, /device:TPU:50, one launch (start us, length us, event | category | flops | bytes accessed | tf_op | source)
XLA Modules:
  0.0 358.4 jit_solution(18192783394693257621)
XLA Ops:
  0.6 0.0 copy-start
  0.6 2.3 collective-permute-start
  2.9 0.9 fusion.2
  3.8 0.7 convert_add_fusion.1
  4.5 3.0 convolution_convert_fusion
  7.5 0.0 collective-permute-done
  7.5 0.1 fusion.3
  7.7 0.0 copy-done
  7.7 1.7 convolution_convert_fusion.1
  9.4 340.9 %shard_map.102 = (bf16[4,48,4096]{2,1,0:T(8,128)(2,1)}, bf16[2048,384]{1,0:T(8,128)(2,1)}, bf16[2048,384]{1,0:T(8,128)(2,1)}, bf16[384,2048]{1,0:T(8,128)(2,1)}) custom-call(bf16[4,48,4096]{2,1,0:T(8,128)(2,1)} %bitcast.25, bf16[4,48,4096]{2,1,0:T(8,128)(2,1)} %bitcast.24, bf16[2048,384]{1,0:T(8,128)(2,1)} %bitcast.30, bf16[2048,384]{1,0:T(8,128)(2,1)} %bitcast.31, ...), custom_call_target="tpu_custom_call" | custom-call | tf_op jit(solution)/shard_map/pallas_call | solution.py:407
  350.3 0.0 copy-start.3
  350.3 3.0 fusion
  353.3 0.0 copy-done.3
  353.3 0.0 copy-start.2
  353.3 1.1 copy.14
  354.5 0.8 copy-done.2
  355.3 0.0 copy-start.1
  355.3 1.1 copy.15
  356.4 0.8 copy-done.1
  357.3 1.1 copy.16
  (1 shorter events, 0.0 us)
Async XLA Ops:
  0.6 7.1 %copy-start = (bf16[1,128,4096]{2,1,0:T(8,128)(2,1)S(1)}, bf16[1,128,4096]{2,1,0:T(8,128)(2,1)}, u32[]{:S(2)}) copy-start(bf16[1,128,4096]{2,1,0:T(8,128)(2,1)} %param.7) | copy-start | bytes 3145732
  0.6 6.9 %collective-permute-start = (s32[128]{0:T(128)}, s32[128]{0:T(128)S(1)}, u32[]{:S(2)}, u32[]{:S(2)}) collective-permute-start(s32[128]{0:T(128)} %bitcast.34), channel_id=1, source_target_pairs={{0,224},{32,192},{64,160},{96,128},{128,96},{160,64},{192,32},{224... | collective-permute-start | bytes 1544 | tf_op jit(solution)/shard_map/ppermute | solution.py:397
  350.3 3.0 copy-start.3
  353.3 2.0 copy-start.2
  355.3 2.0 copy-start.1

commit v2 on v1

--- a/solution.py
+++ b/solution.py
@@ -11,7 +11,9 @@
 CAP = 48
 SHARES = 4
 RING = 8
-STEPS = 9
+STEPS = 12
+LAG = 3
+X_ENTERS = 0
 COLS = 256
 MESH = pl.DeviceIdType.MESH
 F32 = jnp.float32
@@ -57,22 +59,26 @@
         z_in = jnp.where(seg == te, z, te * SHARES + far)
         src, buf, s = ((px, xb, mirror), (pz, zb, sec))[t]
         return remote(
-            src.at[e], buf.at[z, yh], ent_send.at[t, e], rx.at[t, z], (s, ye * RING + z_in, rep)
+            src.at[e], buf.at[z, yh], ent_send.at[t, e], rx.at[t, z, yh], (s, ye * RING + z_in, rep)
         )
 
-    own_copy = [
-        pltpu.make_async_copy(pz.at[e], zb.at[z, yh], rx.at[1, z]) for e in range(EXPERTS)
-    ]
+    def own_copy(e):
+        return pltpu.make_async_copy(pz.at[e], zb.at[z, yh], rx.at[1, z, yh])
+
+    def enter(t):
+        for away in (False, True):
+            for e in range(EXPERTS):
+                go = (e % 2 != seg) if away else (e % 2 == seg)
+
+                @pl.when(go if t == 0 else go & (mine != e))
+                def _():
+                    entry(e, t).start()
+
     for e in range(EXPERTS):
         @pl.when(mine == e)
         def _():
-            own_copy[e].start()
-
-        @pl.when(mine != e)
-        def _():
-            entry(e, 1).start()
-    for e in range(EXPERTS):
-        entry(e, 0).start()
+            own_copy(e).start()
+    enter(1)
 
     rows = pl.ds(pl.multiple_of(rep * half, half), half)
     rows_far = pl.ds(pl.multiple_of(other * half, half), half)
@@ -87,22 +93,22 @@
 
     right, left = here(k + 1), here(k - 1)
 
-    def forward(t, buf, side, zz):
+    def forward(t, zz, y, side):
+        buf = (xb, zb)[t]
         return remote(
-            buf.at[zz], buf.at[zz], fwd_send.at[t, side, zz], rx.at[t, zz], (left, right)[side]
+            buf.at[zz, y], buf.at[zz, y], fwd_send.at[t, side, zz, y], rx.at[t, zz, y], (left, right)[side]
         )
 
-    def arrive(pos, go_left, go_right):
-        zz = zof(pos)
-        for t, buf in ((1, zb), (0, xb)):
-            remote(
-                buf.at[zz], buf.at[zz], fwd_send.at[t, 0, zz], rx.at[t, zz], twin
-            ).wait_recv()
-            for side, go in ((1, go_right), (0, go_left)):
-                if go is not None:
-                    @pl.when(go)
-                    def _():
-                        forward(t, buf, side, zz).start()
+    halves = (yh, 1 - yh)
+
+    def landed(t, zz, y):
+        buf = (xb, zb)[t]
+        remote(buf.at[zz, y], buf.at[zz, y], fwd_send.at[t, 0, zz, y], rx.at[t, zz, y], twin).wait_recv()
+
+    def pass_on(t, zz, y, side):
+        @pl.when(c > 0 if side == 0 else c < SHARES - 1)
+        def _():
+            forward(t, zz, y, side).start()
 
     def compute(zz):
         n_rows = 2 * CAP
@@ -126,33 +132,35 @@
 
         lax.fori_loop(0, width // chunk, part, None)
 
-    def go_back(src, zz, side, at_end):
+    def go_back(src, zz, y, side, at_end):
         slot = jnp.where(at_end, RING, zz) if side else zz
         return remote(
-            src.at[zz], rb.at[slot], rsend.at[0, zz], rr.at[slot], (left, right)[side]
+            src.at[zz, y], rb.at[slot, y], rsend.at[zz, y], rr.at[slot, y], (left, right)[side]
         )
 
     def go_home(src, zz, y):
         return remote(
-            src.at[zz, y], f_out.at[mine], rsend.at[y, zz], fr.at[mine], here(y * RING + zz)
+            src.at[zz, y], f_out.at[mine], rsend.at[zz, y], fr.at[mine], here(y * RING + zz)
         )
 
-    def add_part(zz):
-        for y in range(2):
-            rb[zz, y] = (rb[zz, y].astype(F32) + pb[zz, y].astype(F32)).astype(BF16)
-
-    def wait_back(slot):
-        remote(rb.at[slot], rb.at[slot], rsend.at[0, 0], rr.at[slot], twin).wait_recv()
-
-    def step_conditions(j):
-        in_left = (j >= 1) & (j <= c + 2)
-        in_right = (j >= 1) & (j <= 5 - c)
-        p_from_right = 6 - c - j
-        p_from_left = j - c
-        from_right = (c < 3) & (p_from_right >= -2) & (p_from_right <= c)
-        from_left = (c > 0) & (p_from_left >= c) & (p_from_left <= 5)
-        finish = j == jnp.where((c == 0) | (c == 3), 6, 4)
-        return in_left, in_right, p_from_right, p_from_left, from_right, from_left, finish
+    def add_part(zz, y):
+        rb[zz, y] = (rb[zz, y].astype(F32) + pb[zz, y].astype(F32)).astype(BF16)
+
+    def wait_back(slot, y):
+        remote(rb.at[slot, y], rb.at[slot, y], rsend.at[0, 0], rr.at[slot, y], twin).wait_recv()
+
+    last = STEPS - 1
+
+    def z_moves(j):
+        return (c - j, (j >= 1) & (j <= c + 2)), (c + j, (j >= 1) & (j <= 5 - c))
+
+    def x_moves(j):
+        p_left, p_right = j - LAG - 2 - c, last - j - c
+        return (p_left, (p_left >= -2) & (p_left < c)), (p_right, (p_right <= 5) & (p_right > c))
+
+    def back_moves(j):
+        p_right, p_left = j - last + c, c + last - j
+        return (p_right, (c < 3) & (p_right >= -2) & (p_right <= c)), (p_left, (c > 0) & (p_left <= 5) & (p_left >= c))
 
     def home_copy():
         return pltpu.make_async_copy(pb.at[z, yh], f_out.at[mine], fr.at[mine])
@@ -177,88 +185,109 @@
     send_down = remote(wdn.at[:, rows_far], g2, gsend.at[1], grecv.at[1], twin)
 
     def step(j, _):
-        in_left, in_right, p_r, p_l, from_right, from_left, finish = step_conditions(j)
+        (z_l, z_in_left), (z_r, z_in_right) = z_moves(j)
+        (x_l, x_in_left), (x_r, x_in_right) = x_moves(j)
+        (b_r, from_right), (b_l, from_left) = back_moves(j)
 
         @pl.when(j == 0)
         def _():
-            arrive(c, c > 0, c < 3)
-
-        @pl.when(in_left)
-        def _():
-            arrive(c - j, None, c < 3)
-
-        @pl.when(in_right)
-        def _():
-            arrive(c + j, c > 0, None)
-
-        @pl.when(j == 0)
-        def _():
+            for y in halves:
+                landed(1, z, y)
+                pass_on(1, z, y, 0)
+                pass_on(1, z, y, 1)
+
+        @pl.when(j == X_ENTERS)
+        def _():
+            enter(0)
+
+        for y in halves:
+            for pos, valid, side in ((z_l, z_in_left, 1), (z_r, z_in_right, 0)):
+                @pl.when(valid)
+                def _():
+                    landed(1, zof(pos), y)
+                    pass_on(1, zof(pos), y, side)
+
+        @pl.when(j == LAG)
+        def _():
+            for y in halves:
+                landed(0, z, y)
             for i, (src, dst) in enumerate(w_parts):
                 pltpu.make_async_copy(src, dst(rows), wloc.at[i]).wait()
                 remote(src, dst(rows_far), wsend.at[i], wrecv.at[i], twin).wait_recv()
 
+        for y in halves:
+            for pos, valid, side in ((x_l, x_in_left, 1), (x_r, x_in_right, 0)):
+                @pl.when(valid)
+                def _():
+                    landed(0, zof(pos), y)
+
+                @pl.when(valid | (pos == c))
+                def _():
+                    pass_on(0, zof(pos), y, side)
+
         def side_step(side, _):
-            pos = jnp.where(side == 0, c - j, c + j)
-            valid = jnp.where(side == 0, (j == 0) | in_left, in_right)
+            pos = jnp.where(side == 2, c, jnp.where(side == 0, x_l, x_r))
+            valid = ((side == 0) & x_in_left) | ((side == 1) & x_in_right) | ((side == 2) & (j == LAG))
 
             @pl.when(valid)
             def _():
                 zz = zof(pos)
                 compute(zz)
 
-                @pl.when((j > 0) & (side == 0) & (c == 3))
-                def _():
-                    go_back(pb, zz, 0, False).start()
+                @pl.when((side == 0) & (c == 3))
+                def _():
+                    for y in halves:
+                        go_back(pb, zz, y, 0, False).start()
 
                 @pl.when((side == 1) & (c == 0))
                 def _():
-                    go_back(pb, zz, 1, pos == 1).start()
-
-        lax.fori_loop(0, 2, side_step, None)
-
-        @pl.when(from_right)
-        def _():
-            zz = zof(p_r)
-            wait_back(zz)
-
-            @pl.when(p_r < c)
+                    for y in halves:
+                        go_back(pb, zz, y, 1, pos == 1).start()
+
+        lax.fori_loop(0, 3, side_step, None)
+
+        for y in halves:
+            @pl.when(from_right)
             def _():
-                add_part(zz)
-
-                @pl.when(c > 0)
-                def _():
-                    go_back(rb, zz, 0, False).start()
-
-                @pl.when(c == 0)
-                def _():
-                    for y in range(2):
+                zz = zof(b_r)
+                wait_back(zz, y)
+
+                @pl.when(b_r < c)
+                def _():
+                    add_part(zz, y)
+
+                    @pl.when(c > 0)
+                    def _():
+                        go_back(rb, zz, y, 0, False).start()
+
+                    @pl.when(c == 0)
+                    def _():
                         go_home(rb, zz, y).start()
 
-        @pl.when(from_left)
-        def _():
-            zz = zof(p_l)
-
-            @pl.when(p_l == c)
+            @pl.when(from_left)
             def _():
-                wait_back(RING)
-
-            @pl.when(p_l > c)
-            def _():
-                wait_back(zz)
-                add_part(zz)
-
-                @pl.when(c < 3)
-                def _():
-                    go_back(rb, zz, 1, p_l == c + 1).start()
-
-                @pl.when(c == 3)
-                def _():
-                    for y in range(2):
+                zz = zof(b_l)
+
+                @pl.when(b_l == c)
+                def _():
+                    wait_back(RING, y)
+
+                @pl.when(b_l > c)
+                def _():
+                    wait_back(zz, y)
+                    add_part(zz, y)
+
+                    @pl.when(c < 3)
+                    def _():
+                        go_back(rb, zz, y, 1, b_l == c + 1).start()
+
+                    @pl.when(c == 3)
+                    def _():
                         go_home(rb, zz, y).start()
 
-        @pl.when(finish)
-        def _():
-            for y in range(2):
+        @pl.when(j == last)
+        def _():
+            for y in (1 - yh, yh):
                 @pl.when(c == 0)
                 def _():
                     pb[z, y] = (pb[z, y].astype(F32) + rb[z, y].astype(F32)).astype(BF16)
@@ -272,25 +301,22 @@
                     total = pb[z, y].astype(F32) + rb[z, y].astype(F32)
                     pb[z, y] = (total + rb[RING, y].astype(F32)).astype(BF16)
 
+                @pl.when(y != yh)
+                def _():
+                    go_home(pb, z, y).start()
+
             home_copy().start()
-            go_home(pb, z, 1 - yh).start()
-
-        @pl.when(j == 5)
+
+        @pl.when(j == last - 1)
         def _():
             lax.fori_loop(other * per_half, (other + 1) * per_half, grads_in, None)
             send_in.start()
 
-        @pl.when(j == 6)
-        def _():
-            lax.fori_loop(other * per_half, (other + 1) * per_half, grads_down, None)
-            send_down.start()
-            lax.fori_loop(rep * per_half, (rep + 1) * per_half, grads_in, None)
-
-        @pl.when(j == 7)
-        def _():
-            lax.fori_loop(rep * per_half, (rep + 1) * per_half, grads_down, None)
-
     lax.fori_loop(0, STEPS, step, None)
+    lax.fori_loop(other * per_half, (other + 1) * per_half, grads_down, None)
+    send_down.start()
+    lax.fori_loop(rep * per_half, (rep + 1) * per_half, grads_in, None)
+    lax.fori_loop(rep * per_half, (rep + 1) * per_half, grads_down, None)
 
     piece = 512
 
@@ -334,48 +360,29 @@
     send_down.wait_send()
 
     def drain(j, _):
-        in_left, in_right, p_r, p_l, from_right, from_left, finish = step_conditions(j)
-
-        def forwarded(go, side, pos):
+        (z_l, z_in_left), (z_r, z_in_right) = z_moves(j)
+        (x_l, x_in_left), (x_r, x_in_right) = x_moves(j)
+        (b_r, from_right), (b_l, from_left) = back_moves(j)
+
+        def sent(go, copy):
             @pl.when(go)
             def _():
-                for t, buf in ((1, zb), (0, xb)):
-                    forward(t, buf, side, zof(pos)).wait_send()
-
-        forwarded(((j == 0) | in_left) & (c < 3), 1, c - j)
-        forwarded(((j == 0) | in_right) & (c > 0), 0, c + j)
-
-        @pl.when(in_left & (c == 3))
-        def _():
-            go_back(pb, zof(c - j), 0, False).wait_send()
-
-        @pl.when(in_right & (c == 0))
-        def _():
-            go_back(pb, zof(c + j), 1, False).wait_send()
-
-        @pl.when(from_right & (p_r < c) & (c > 0))
-        def _():
-            go_back(rb, zof(p_r), 0, False).wait_send()
-
-        @pl.when(from_right & (p_r < c) & (c == 0))
-        def _():
-            for y in range(2):
-                go_home(rb, zof(p_r), y).wait_send()
-
-        @pl.when(from_left & (p_l > c) & (c < 3))
-        def _():
-            go_back(rb, zof(p_l), 1, False).wait_send()
-
-        @pl.when(from_left & (p_l > c) & (c == 3))
-        def _():
-            for y in range(2):
-                go_home(rb, zof(p_l), y).wait_send()
-
-        @pl.when(finish)
-        def _():
-            go_home(pb, z, 1 - yh).wait_send()
+                copy().wait_send()
+
+        for y in halves:
+            sent((z_in_left | (j == 0)) & (c < 3), lambda: forward(1, zof(z_l), y, 1))
+            sent((z_in_right | (j == 0)) & (c > 0), lambda: forward(1, zof(z_r), y, 0))
+            sent((x_in_left | (x_l == c)) & (c < 3), lambda: forward(0, zof(x_l), y, 1))
+            sent((x_in_right | (x_r == c)) & (c > 0), lambda: forward(0, zof(x_r), y, 0))
+            sent(x_in_left & (c == 3), lambda: go_back(pb, zof(x_l), y, 0, False))
+            sent(x_in_right & (c == 0), lambda: go_back(pb, zof(x_r), y, 1, False))
+            sent(from_right & (b_r < c) & (c > 0), lambda: go_back(rb, zof(b_r), y, 0, False))
+            sent(from_left & (b_l > c) & (c < 3), lambda: go_back(rb, zof(b_l), y, 1, False))
+            sent(from_right & (b_r < c) & (c == 0), lambda: go_home(rb, zof(b_r), y))
+            sent(from_left & (b_l > c) & (c == 3), lambda: go_home(rb, zof(b_l), y))
 
     lax.fori_loop(0, STEPS, drain, None)
+    go_home(pb, z, 1 - yh).wait_send()
     for out in outs:
         out.wait()
 
@@ -425,11 +432,11 @@
             pltpu.VMEM((RING, 2 * CAP, units), BF16),
             pltpu.VMEM((half, 2 * units), BF16),
             pltpu.VMEM((units, half), BF16),
-            dma((2, RING)),
+            dma((2, RING, 2)),
             dma((2, EXPERTS)),
-            dma((2, 2, RING)),
-            dma((RING + 1,)),
-            dma((2, RING)),
+            dma((2, 2, RING, 2)),
+            dma((RING + 1, 2)),
+            dma((RING, 2)),
             dma((EXPERTS,)),
             dma((3,)),
             dma((3,)),

time: 359 us -> 305 us (0.85)
  the two profiles are of different devices: /device:TPU:50 before, /device:TPU:30 now
where the time goes in v2:
time: 305 us
  Pallas kernels  288 us (94%)
  matrix products  8.73 us (3%)
  local copies, waits for them, and re-layouts  5.11 us (2%)
    pallas_call x1, Pallas kernels, body(): pl.pallas_call(kernel, out_shape=(jax.ShapeDtypeStruct((EXPERTS, CAP, wid...  288 us
    dot_general x5, matrix products, dot(): lax.dot_general(a, b, (((dim_a,), (dim_b,)), ((), ())), preferred_element...  8.73 us
  transfers between devices with their start and end apart: 1, of which 1 were waited for; matrix products, arithmetic and copies ran while one was open for 1% of the time, Pallas kernels for 0%

profile of v2, /device:TPU:30, one launch (start us, length us, event | category | flops | bytes accessed | tf_op | source)
XLA Modules:
  0.0 304.6 jit_solution(13257007693285545466)
XLA Ops:
  0.6 0.0 copy-start
  0.6 0.7 collective-permute-start
  1.4 0.9 fusion.2
  2.3 0.7 convert_add_fusion.1
  2.9 3.0 convolution_convert_fusion
  6.0 0.6 collective-permute-done
  6.5 0.1 fusion.3
  6.7 0.0 copy-done
  6.7 1.7 convolution_convert_fusion.1
  8.4 288.1 %shard_map.102 = (bf16[4,48,4096]{2,1,0:T(8,128)(2,1)}, bf16[2048,384]{1,0:T(8,128)(2,1)}, bf16[2048,384]{1,0:T(8,128)(2,1)}, bf16[384,2048]{1,0:T(8,128)(2,1)}) custom-call(bf16[4,48,4096]{2,1,0:T(8,128)(2,1)} %bitcast.25, bf16[4,48,4096]{2,1,0:T(8,128)(2,1)} %bitcast.24, bf16[2048,384]{1,0:T(8,128)(2,1)} %bitcast.30, bf16[2048,384]{1,0:T(8,128)(2,1)} %bitcast.31, ...), custom_call_target="tpu_custom_call" | custom-call | tf_op jit(solution)/shard_map/pallas_call | solution.py:414
  296.5 0.0 copy-start.3
  296.5 3.0 fusion
  299.5 0.0 copy-done.3
  299.5 0.0 copy-start.2
  299.5 1.1 copy.14
  300.6 0.8 copy-done.2
  301.5 0.0 copy-start.1
  301.5 1.1 copy.15
  302.6 0.8 copy-done.1
  303.4 1.1 copy.16
  (1 shorter events, 0.0 us)
Async XLA Ops:
  0.6 6.1 %copy-start = (bf16[1,128,4096]{2,1,0:T(8,128)(2,1)S(1)}, bf16[1,128,4096]{2,1,0:T(8,128)(2,1)}, u32[]{:S(2)}) copy-start(bf16[1,128,4096]{2,1,0:T(8,128)(2,1)} %param.7) | copy-start | bytes 3145732
  0.6 5.9 %collective-permute-start = (s32[128]{0:T(128)}, s32[128]{0:T(128)S(1)}, u32[]{:S(2)}, u32[]{:S(2)}) collective-permute-start(s32[128]{0:T(128)} %bitcast.34), channel_id=1, source_target_pairs={{0,224},{32,192},{64,160},{96,128},{128,96},{160,64},{192,32},{224... | collective-permute-start | bytes 1544 | tf_op jit(solution)/shard_map/ppermute | solution.py:404
  296.5 3.0 copy-start.3
  299.5 2.0 copy-start.2
  301.5 2.0 copy-start.1

commit v3 on v2

--- a/solution.py
+++ b/solution.py
@@ -13,7 +13,6 @@
 RING = 8
 STEPS = 12
 LAG = 3
-X_ENTERS = 0
 COLS = 256
 MESH = pl.DeviceIdType.MESH
 F32 = jnp.float32
@@ -24,11 +23,28 @@
     return lax.dot_general(a, b, (((dim_a,), (dim_b,)), ((), ())), preferred_element_type=F32)
 
 
+def slots_of(chosen):
+    n_tok = chosen.shape[1]
+    experts = lax.broadcasted_iota(jnp.int32, (8, n_tok), 0)
+    choose = jnp.where(experts == chosen, 1.0, 0.0)
+    earlier = lax.broadcasted_iota(jnp.int32, (n_tok, n_tok), 0) < lax.broadcasted_iota(
+        jnp.int32, (n_tok, n_tok), 1
+    )
+    before = dot(choose.astype(BF16), jnp.where(earlier, 1.0, 0.0).astype(BF16), 1, 0)
+    slot = jnp.sum(choose * before, axis=0, keepdims=True).astype(jnp.int32)
+    return jnp.broadcast_to(chosen * CAP + slot, (8, n_tok))
+
+
+def places(row):
+    ids = lax.broadcasted_iota(jnp.int32, (EXPERTS * CAP, row.shape[1]), 0)
+    return jnp.where(ids == row, 1.0, 0.0).astype(BF16)
+
+
 def kernel(
-    px, pz, wg, wu, wd,
+    rows_in, rows_out, weight, chosen, wg, wu, wd,
     f_out, gg_out, gu_out, gd_out,
-    xb, zb, wgu, wdn, pb, rb, d2, hd, g1, g2,
-    rx, ent_send, fwd_send, rr, rsend, fr, wrecv, wsend, wloc, grecv, gsend, gloc,
+    px, pz, target, far_target, xb, zb, wgu, wdn, pb, rb, d2, hd, g1, g2,
+    tsem, rx, ent_send, fwd_send, rr, rsend, fr, wrecv, wsend, wloc, grecv, gsend, gloc,
 ):
     sec, k, rep = lax.axis_index("section"), lax.axis_index("expert"), lax.axis_index("dp")
     mirror = lax.axis_size("section") - 1 - sec
@@ -74,10 +90,61 @@
                 def _():
                     entry(e, t).start()
 
+    bar = pltpu.get_barrier_semaphore()
+
+    def greet(*dev):
+        pl.semaphore_signal(bar, inc=1, device_id=dev, device_id_type=MESH)
+
+    z_far = (1 - seg) * SHARES + jnp.where(c < 2, SHARES - 1, 0)
+    step_far = jnp.where(c == 0, RING - 1, 1)
+    at_end = (c == 0) | (c == SHARES - 1)
+    greet(*twin)
+    greet(sec, (1 - yh) * RING + z, rep)
+    for ye in range(2):
+        greet(sec, ye * RING + z_far, rep)
+        greet(mirror, ye * RING + z, rep)
+        greet(mirror, ye * RING + z_far, rep)
+
+        @pl.when(at_end)
+        def _():
+            z_two = (z + 2 * step_far) % RING
+            greet(sec, ye * RING + z_two, rep)
+            greet(mirror, ye * RING + z_two, rep)
+
+    @pl.when(c > 0)
+    def _():
+        greet(*here(k - 1))
+
+    @pl.when(c < SHARES - 1)
+    def _():
+        greet(*here(k + 1))
+
+    def pack(out, row, src, scale):
+        placing = places(row)
+        factor = None
+        if scale is not None:
+            factor = jnp.sum(placing.astype(F32) * scale, axis=1, keepdims=True)
+        chunk = 1024
+
+        def one(n, _):
+            cols = pl.ds(pl.multiple_of(n * chunk, chunk), chunk)
+            got = dot(placing, src[:, cols], 1, 0)
+            if factor is not None:
+                got = factor * got
+            out[:, :, cols] = got.astype(BF16).reshape(EXPERTS, CAP, chunk)
+
+        lax.fori_loop(0, width // chunk, one, None)
+
+    target[...] = slots_of(chosen[...])
+    pack(pz, target[0:1, :], rows_out, weight[...])
+    pl.semaphore_wait(bar, jnp.where(at_end, 13, 10))
+
     for e in range(EXPERTS):
         @pl.when(mine == e)
         def _():
             own_copy(e).start()
+    send_target = remote(target, far_target, tsem.at[0], tsem.at[1], (mirror, k, rep))
+    send_target.start()
     enter(1)
 
     rows = pl.ds(pl.multiple_of(rep * half, half), half)
@@ -91,6 +158,10 @@
         pltpu.make_async_copy(src, dst(rows), wloc.at[i]).start()
         remote(src, dst(rows), wsend.at[i], wrecv.at[i], twin).start()
 
+    send_target.wait_recv()
+    pack(px, far_target[0:1, :], rows_in, None)
+    enter(0)
+
     right, left = here(k + 1), here(k - 1)
 
     def forward(t, zz, y, side):
@@ -100,6 +171,7 @@
         )
 
     halves = (yh, 1 - yh)
+    backward = (1 - yh, yh)
 
     def landed(t, zz, y):
         buf = (xb, zb)[t]
@@ -196,10 +268,6 @@
                 pass_on(1, z, y, 0)
                 pass_on(1, z, y, 1)
 
-        @pl.when(j == X_ENTERS)
-        def _():
-            enter(0)
-
         for y in halves:
             for pos, valid, side in ((z_l, z_in_left, 1), (z_r, z_in_right, 0)):
                 @pl.when(valid)
@@ -236,17 +304,17 @@
 
                 @pl.when((side == 0) & (c == 3))
                 def _():
-                    for y in halves:
+                    for y in backward:
                         go_back(pb, zz, y, 0, False).start()
 
                 @pl.when((side == 1) & (c == 0))
                 def _():
-                    for y in halves:
+                    for y in backward:
                         go_back(pb, zz, y, 1, pos == 1).start()
 
         lax.fori_loop(0, 3, side_step, None)
 
-        for y in halves:
+        for y in backward:
             @pl.when(from_right)
             def _():
                 zz = zof(b_r)
@@ -285,9 +353,8 @@
                     def _():
                         go_home(rb, zz, y).start()
 
-        @pl.when(j == last)
-        def _():
-            for y in (1 - yh, yh):
+            @pl.when(j == last)
+            def _():
                 @pl.when(c == 0)
                 def _():
                     pb[z, y] = (pb[z, y].astype(F32) + rb[z, y].astype(F32)).astype(BF16)
@@ -301,22 +368,21 @@
                     total = pb[z, y].astype(F32) + rb[z, y].astype(F32)
                     pb[z, y] = (total + rb[RING, y].astype(F32)).astype(BF16)
 
-                @pl.when(y != yh)
-                def _():
+                if y is yh:
+                    home_copy().start()
+                else:
                     go_home(pb, z, y).start()
-
-            home_copy().start()
 
         @pl.when(j == last - 1)
         def _():
             lax.fori_loop(other * per_half, (other + 1) * per_half, grads_in, None)
             send_in.start()
+            lax.fori_loop(other * per_half, (other + 1) * per_half, grads_down, None)
+            send_down.start()
+            lax.fori_loop(rep * per_half, (rep + 1) * per_half, grads_in, None)
+            lax.fori_loop(rep * per_half, (rep + 1) * per_half, grads_down, None)
 
     lax.fori_loop(0, STEPS, step, None)
-    lax.fori_loop(other * per_half, (other + 1) * per_half, grads_down, None)
-    send_down.start()
-    lax.fori_loop(rep * per_half, (rep + 1) * per_half, grads_in, None)
-    lax.fori_loop(rep * per_half, (rep + 1) * per_half, grads_down, None)
 
     piece = 512
 
@@ -356,6 +422,7 @@
             entry(e, 1).wait_send()
     for i, (src, dst) in enumerate(w_parts):
         remote(src, dst(rows), wsend.at[i], wrecv.at[i], twin).wait_send()
+    send_target.wait_send()
     send_in.wait_send()
     send_down.wait_send()
 
@@ -387,41 +454,38 @@
         out.wait()
 
 
-def placing_of(chosen):
-    n_tok = chosen.shape[0]
-    choose = chosen[:, None] == jnp.arange(EXPERTS, dtype=jnp.int32)[None, :]
-    tok = jnp.arange(n_tok, dtype=jnp.int32)
-    lower = (tok[:, None] > tok[None, :]).astype(BF16)
-    before = dot(lower, choose.astype(BF16), 1, 0)
-    slot = jnp.sum(jnp.where(choose, before, 0.0), axis=1).astype(jnp.int32)
-    target = chosen * CAP + slot
-    return (jnp.arange(EXPERTS * CAP, dtype=jnp.int32)[:, None] == target[None, :]).astype(BF16)
+def finish_kernel(merged, chosen, gg, gu, gd, gi_out, gg_out, gu_out, gd_out):
+    placing = places(slots_of(chosen[...])[0:1, :])
+    gi_out[...] = dot(placing, merged[...], 0, 0).astype(BF16)
+    gg_out[...] = gg[...]
+    gu_out[...] = gu[...]
+    gd_out[...] = gd[...]
 
 
 def body(saved_rows, grad_out, expert_ids, combine, w_gate, w_up, w_down):
-    n_sec = lax.axis_size("section")
-    chosen = expert_ids[0, :, 0]
-    chosen_far = lax.ppermute(chosen, "section", [(i, n_sec - 1 - i) for i in range(n_sec)])
-    width = saved_rows.shape[2]
+    tokens, width = saved_rows.shape[1:]
     units = w_gate.shape[2]
-    placing = placing_of(chosen)
-    scaled = (combine[0] * grad_out[0].astype(F32)).astype(BF16)
-    pz = dot(placing, scaled, 1, 0).astype(BF16).reshape(EXPERTS, CAP, width)
-    px = dot(placing_of(chosen_far), saved_rows[0], 1, 0).astype(BF16)
-    px = px.reshape(EXPERTS, CAP, width)
     half = width // 2
+    chosen = expert_ids.reshape(1, tokens)
+    weight = combine.reshape(1, tokens)
     dma = pltpu.SemaphoreType.DMA
-    outs = pl.pallas_call(
+    anywhere = pl.BlockSpec(memory_space=pl.ANY)
+    in_vmem = pl.BlockSpec(memory_space=pltpu.VMEM)
+    grad_shapes = (
+        jax.ShapeDtypeStruct((half, units), BF16),
+        jax.ShapeDtypeStruct((half, units), BF16),
+        jax.ShapeDtypeStruct((units, half), BF16),
+    )
+    merged, *grads = pl.pallas_call(
         kernel,
-        out_shape=(
-            jax.ShapeDtypeStruct((EXPERTS, CAP, width), BF16),
-            jax.ShapeDtypeStruct((half, units), BF16),
-            jax.ShapeDtypeStruct((half, units), BF16),
-            jax.ShapeDtypeStruct((units, half), BF16),
-        ),
-        in_specs=[pl.BlockSpec(memory_space=pl.ANY)] * 5,
-        out_specs=[pl.BlockSpec(memory_space=pl.ANY)] * 4,
+        out_shape=(jax.ShapeDtypeStruct((EXPERTS, CAP, width), BF16),) + grad_shapes,
+        in_specs=[in_vmem] * 4 + [anywhere] * 3,
+        out_specs=[anywhere] * 4,
         scratch_shapes=[
+            pltpu.VMEM((EXPERTS, CAP, width), BF16),
+            pltpu.VMEM((EXPERTS, CAP, width), BF16),
+            pltpu.VMEM((8, tokens), jnp.int32),
+            pltpu.VMEM((8, tokens), jnp.int32),
             pltpu.VMEM((RING, 2, CAP, width), BF16),
             pltpu.VMEM((RING, 2, CAP, width), BF16),
             pltpu.VMEM((width, 2 * units), BF16),
@@ -432,6 +496,7 @@
             pltpu.VMEM((RING, 2 * CAP, units), BF16),
             pltpu.VMEM((half, 2 * units), BF16),
             pltpu.VMEM((units, half), BF16),
+            dma((2,)),
             dma((2, RING, 2)),
             dma((2, EXPERTS)),
             dma((2, 2, RING, 2)),
@@ -446,12 +511,26 @@
             dma((3,)),
         ],
         compiler_params=pltpu.CompilerParams(
-            has_side_effects=True, vmem_limit_bytes=60 * 1024 * 1024
+            collective_id=0, has_side_effects=True, vmem_limit_bytes=60 * 1024 * 1024
         ),
-    )(px, pz, w_gate[0], w_up[0], w_down[0])
-    merged, grad_gate, grad_up, grad_down = outs
-    grad_in = dot(placing, merged.reshape(EXPERTS * CAP, width), 0, 0).astype(BF16)
-    return grad_in[None], grad_gate[None], grad_up[None], grad_down[None]
+    )(saved_rows[0], grad_out[0], weight, chosen, w_gate[0], w_up[0], w_down[0])
+    steps = 2
+    slots = EXPERTS * CAP
+    row_spec = pl.BlockSpec((half // steps, units), lambda i: (i, 0))
+    grad_specs = [row_spec, row_spec, pl.BlockSpec((units // steps, half), lambda i: (i, 0))]
+    grad_in, *grads = pl.pallas_call(
+        finish_kernel,
+        grid=(steps,),
+        out_shape=(jax.ShapeDtypeStruct((tokens, width), BF16),) + grad_shapes,
+        in_specs=[
+            pl.BlockSpec((slots, width // steps), lambda i: (0, i)),
+            pl.BlockSpec((1, tokens), lambda i: (0, 0)),
+        ]
+        + grad_specs,
+        out_specs=[pl.BlockSpec((tokens, width // steps), lambda i: (0, i))] + grad_specs,
+        compiler_params=pltpu.CompilerParams(vmem_limit_bytes=60 * 1024 * 1024),
+    )(merged.reshape(slots, width), chosen, *grads)
+    return grad_in[None], *(grad[None] for grad in grads)
 
 
 def solution(mesh):

time: 305 us -> 295 us (0.967); the launches traced: 305 us -> 290 us
  matrix products: 8.73 us -> 0 us
  local copies, waits for them, and re-layouts: 5.11 us -> 0 us
    dot_general x5 -> x0, matrix products: 8.73 us -> none  [dot(): lax.dot_general(a, b, (((dim_a,), (dim_b,)), ((), ())), preferred_element...]
    unnamed x11 -> x0, local copies, waits for them, and re-layouts: 5.11 us -> none
    pallas_call x0 -> x1, Pallas kernels: none -> 4.86 us  [body(): pl.pallas_call(finish_kernel, grid=(steps,), out_shape=(jax.ShapeDtypeStr...]
    pallas_call x1, Pallas kernels: 288 us -> 285 us  [body(): pl.pallas_call(kernel, out_shape=(jax.ShapeDtypeStruct((EXPERTS, CAP, wid...]
  transfers between devices with their start and end apart: 1 -> 0, of which waited for: 1 -> 0; matrix products, arithmetic and copies ran while one was open for 1% -> 0% of each run, Pallas kernels for 0% -> 0%
where the time goes in v3:
time: 295 us; the launch traced here: 290 us
  Pallas kernels  290 us (98%)
    pallas_call x1, Pallas kernels, body(): pl.pallas_call(kernel, out_shape=(jax.ShapeDtypeStruct((EXPERTS, CAP, wid...  285 us

profile of v3, /device:TPU:30, one launch (start us, length us, event | category | flops | bytes accessed | tf_op | source)
XLA Modules:
  0.0 290.4 jit_solution(8143675480008406024)
XLA Ops:
  0.6 284.9 %shard_map.102 = (bf16[4,48,4096]{2,1,0:T(8,128)(2,1)}, bf16[2048,384]{1,0:T(8,128)(2,1)}, bf16[2048,384]{1,0:T(8,128)(2,1)}, bf16[384,2048]{1,0:T(8,128)(2,1)}) custom-call(bf16[128,4096]{1,0:T(8,128)(2,1)} %bitcast.16, bf16[128,4096]{1,0:T(8,128)(2,1)} %bitcast.17, f32[1,128]{1,0:T(1,128)} %bitcast.20, s32[1,128]{1,0:T(1,128)} %bitcast.18, ...), custom_call_target="tpu_custom_call" | custom-call | tf_op jit(solution)/shard_map/pallas_call | solution.py:479
  285.5 4.9 %shard_map.103 = (bf16[128,4096]{1,0:T(8,128)(2,1)}, bf16[2048,384]{1,0:T(8,128)(2,1)}, bf16[2048,384]{1,0:T(8,128)(2,1)}, bf16[384,2048]{1,0:T(8,128)(2,1)}) custom-call(bf16[192,4096]{1,0:T(8,128)(2,1)} %bitcast.15, s32[1,128]{1,0:T(1,128)} %bitcast.19, bf16[2048,384]{1,0:T(8,128)(2,1)} %get-tuple-element.13.gg, bf16[2048,384]{1,0:T(8,128)(2,1)} %get-tuple-element.14.gu, ...), custom_call_target="tpu_custom_call" | custom-call | tf_op jit(solution)/shard_map/pallas_call | solution.py:521

commit v4 on v3

--- a/solution.py
+++ b/solution.py
@@ -11,8 +11,9 @@
 CAP = 48
 SHARES = 4
 RING = 8
-STEPS = 12
 LAG = 3
+X_LAST = LAG + 8
+STEPS = X_LAST + 2
 COLS = 256
 MESH = pl.DeviceIdType.MESH
 F32 = jnp.float32
@@ -35,16 +36,16 @@
     return jnp.broadcast_to(chosen * CAP + slot, (8, n_tok))
 
 
-def places(row):
-    ids = lax.broadcasted_iota(jnp.int32, (EXPERTS * CAP, row.shape[1]), 0)
+def places(row, slots=EXPERTS * CAP):
+    ids = lax.broadcasted_iota(jnp.int32, (slots, row.shape[1]), 0)
     return jnp.where(ids == row, 1.0, 0.0).astype(BF16)
 
 
 def kernel(
     rows_in, rows_out, weight, chosen, wg, wu, wd,
     f_out, gg_out, gu_out, gd_out,
-    px, pz, target, far_target, xb, zb, wgu, wdn, pb, rb, d2, hd, g1, g2,
-    tsem, rx, ent_send, fwd_send, rr, rsend, fr, wrecv, wsend, wloc, grecv, gsend, gloc,
+    px, pz, pn, raw, target, far_target, near_target, xb, zb, wgu, wdn, pb, rb, d2, hd, g1, g2,
+    tsem, raw_send, raw_recv, rx, ent_send, fwd_send, rr, rsend, fr, wrecv, wsend, wloc, grecv, gsend, gloc,
 ):
     sec, k, rep = lax.axis_index("section"), lax.axis_index("expert"), lax.axis_index("dp")
     mirror = lax.axis_size("section") - 1 - sec
@@ -69,47 +70,59 @@
             src_ref=src, dst_ref=dst, send_sem=send, recv_sem=recv, device_id=dev, device_id_type=MESH
         )
 
-    def entry(e, t):
+    pair = z + 1 - 2 * (z % 2)
+    z_far = (1 - seg) * SHARES + jnp.where(c < 2, SHARES - 1, 0)
+    at_end = (c == 0) | (c == SHARES - 1)
+    inner = (c > 0) & (c < SHARES - 1)
+
+    def entry(e, t, proxy):
         ye, te = e // 2, e % 2
-        far = jnp.where(c < 2, SHARES - 1, 0)
-        z_in = jnp.where(seg == te, z, te * SHARES + far)
-        src, buf, s = ((px, xb, mirror), (pz, zb, sec))[t]
+        z_in = jnp.where(seg == te, z, z_far)
+        src = pn.at[t] if proxy else (px, pz)[t]
+        to = sec if proxy or t == 1 else mirror
+        slot = pair if proxy else z
         return remote(
-            src.at[e], buf.at[z, yh], ent_send.at[t, e], rx.at[t, z, yh], (s, ye * RING + z_in, rep)
+            src.at[e], (xb, zb)[t].at[slot, yh], ent_send.at[proxy, t, e], rx.at[t, slot, yh],
+            (to, ye * RING + z_in, rep),
         )
 
-    def own_copy(e):
-        return pltpu.make_async_copy(pz.at[e], zb.at[z, yh], rx.at[1, z, yh])
-
-    def enter(t):
+    def entries(t, proxy, act):
         for away in (False, True):
             for e in range(EXPERTS):
-                go = (e % 2 != seg) if away else (e % 2 == seg)
-
-                @pl.when(go if t == 0 else go & (mine != e))
-                def _():
-                    entry(e, t).start()
+                go = (seg != e % 2) & at_end if away else seg == e % 2
+
+                @pl.when(go if t == 0 and not proxy else go & (mine != e))
+                def _():
+                    act(entry(e, t, proxy))
+
+    def own_copy(e, t, proxy):
+        slot = pair if proxy else z
+        src = pn.at[t] if proxy else pz
+        return pltpu.make_async_copy(src.at[e], (xb, zb)[t].at[slot, yh], rx.at[t, slot, yh])
+
+    def keep(t, proxy):
+        for e in range(EXPERTS):
+            @pl.when(mine == e)
+            def _():
+                own_copy(e, t, proxy).start()
 
     bar = pltpu.get_barrier_semaphore()
 
     def greet(*dev):
         pl.semaphore_signal(bar, inc=1, device_id=dev, device_id_type=MESH)
 
-    z_far = (1 - seg) * SHARES + jnp.where(c < 2, SHARES - 1, 0)
     step_far = jnp.where(c == 0, RING - 1, 1)
-    at_end = (c == 0) | (c == SHARES - 1)
     greet(*twin)
     greet(sec, (1 - yh) * RING + z, rep)
+    greet(mirror, yh * RING + pair, rep)
     for ye in range(2):
         greet(sec, ye * RING + z_far, rep)
         greet(mirror, ye * RING + z, rep)
-        greet(mirror, ye * RING + z_far, rep)
 
         @pl.when(at_end)
         def _():
-            z_two = (z + 2 * step_far) % RING
-            greet(sec, ye * RING + z_two, rep)
-            greet(mirror, ye * RING + z_two, rep)
+            greet(sec, ye * RING + (z + 2 * step_far) % RING, rep)
+            greet(mirror, ye * RING + z_far, rep)
 
     @pl.when(c > 0)
     def _():
@@ -119,8 +132,7 @@
     def _():
         greet(*here(k + 1))
 
-    def pack(out, row, src, scale):
-        placing = places(row)
+    def pack(out, placing, src, scale):
         factor = None
         if scale is not None:
             factor = jnp.sum(placing.astype(F32) * scale, axis=1, keepdims=True)
@@ -131,21 +143,50 @@
             got = dot(placing, src[:, cols], 1, 0)
             if factor is not None:
                 got = factor * got
-            out[:, :, cols] = got.astype(BF16).reshape(EXPERTS, CAP, chunk)
+            got = got.astype(BF16)
+            out[..., cols] = got.reshape(out.shape[:-1] + (chunk,))
 
         lax.fori_loop(0, width // chunk, one, None)
 
     target[...] = slots_of(chosen[...])
-    pack(pz, target[0:1, :], rows_out, weight[...])
-    pl.semaphore_wait(bar, jnp.where(at_end, 13, 10))
-
-    for e in range(EXPERTS):
-        @pl.when(mine == e)
-        def _():
-            own_copy(e).start()
+    n_tok = raw.shape[1]
+
+    @pl.when(inner)
+    def _():
+        tokens = lax.broadcasted_iota(jnp.int32, (1, n_tok), 1)
+        pack(raw.at[1], places(tokens, n_tok), rows_out, weight[...])
+
+    pack(pz, places(target[0:1, :]), rows_out, weight[...])
+    pl.semaphore_wait(bar, jnp.where(at_end, 12, 9))
+
+    near = here(yh * RING + pair)
+    raw_copies = (
+        remote(target, near_target, raw_send.at[0], raw_recv.at[0], near),
+        remote(raw.at[1], raw.at[1], raw_send.at[1], raw_recv.at[1], near),
+        remote(rows_in, raw.at[0], raw_send.at[2], raw_recv.at[2], (mirror, yh * RING + pair, rep)),
+    )
+    keep(1, 0)
     send_target = remote(target, far_target, tsem.at[0], tsem.at[1], (mirror, k, rep))
     send_target.start()
-    enter(1)
+
+    @pl.when(inner)
+    def _():
+        raw_copies[0].start()
+        raw_copies[1].start()
+
+    entries(1, 0, lambda copy: copy.start())
+
+    @pl.when(inner)
+    def _():
+        raw_copies[2].start()
+
+    def enter_near(t):
+        if t == 1:
+            raw_copies[0].wait_recv()
+        raw_copies[2 - t].wait_recv()
+        pack(pn.at[t], places(near_target[0:1, :]), raw.at[t], None)
+        keep(t, 1)
+        entries(t, 1, lambda copy: copy.start())
 
     rows = pl.ds(pl.multiple_of(rep * half, half), half)
     rows_far = pl.ds(pl.multiple_of(other * half, half), half)
@@ -159,8 +200,8 @@
         remote(src, dst(rows), wsend.at[i], wrecv.at[i], twin).start()
 
     send_target.wait_recv()
-    pack(px, far_target[0:1, :], rows_in, None)
-    enter(0)
+    pack(px, places(far_target[0:1, :]), rows_in, None)
+    entries(0, 0, lambda copy: copy.start())
 
     right, left = here(k + 1), here(k - 1)
 
@@ -177,10 +218,8 @@
         buf = (xb, zb)[t]
         remote(buf.at[zz, y], buf.at[zz, y], fwd_send.at[t, 0, zz, y], rx.at[t, zz, y], twin).wait_recv()
 
-    def pass_on(t, zz, y, side):
-        @pl.when(c > 0 if side == 0 else c < SHARES - 1)
-        def _():
-            forward(t, zz, y, side).start()
+    onward = (c > 0, c < SHARES - 1)
+    own_onward = (c >= 2, c <= 1)
 
     def compute(zz):
         n_rows = 2 * CAP
@@ -227,7 +266,7 @@
         return (c - j, (j >= 1) & (j <= c + 2)), (c + j, (j >= 1) & (j <= 5 - c))
 
     def x_moves(j):
-        p_left, p_right = j - LAG - 2 - c, last - j - c
+        p_left, p_right = j - LAG - 2 - c, X_LAST - j - c
         return (p_left, (p_left >= -2) & (p_left < c)), (p_right, (p_right <= 5) & (p_right > c))
 
     def back_moves(j):
@@ -265,15 +304,22 @@
         def _():
             for y in halves:
                 landed(1, z, y)
-                pass_on(1, z, y, 0)
-                pass_on(1, z, y, 1)
+                for side in range(2):
+                    @pl.when(own_onward[side])
+                    def _():
+                        forward(1, z, y, side).start()
 
         for y in halves:
             for pos, valid, side in ((z_l, z_in_left, 1), (z_r, z_in_right, 0)):
-                @pl.when(valid)
+                @pl.when(valid & onward[side])
                 def _():
                     landed(1, zof(pos), y)
-                    pass_on(1, zof(pos), y, side)
+                    forward(1, zof(pos), y, side).start()
+
+        for t in (1, 0):
+            @pl.when((j == 2 - t) & at_end)
+            def _():
+                enter_near(t)
 
         @pl.when(j == LAG)
         def _():
@@ -289,9 +335,13 @@
                 def _():
                     landed(0, zof(pos), y)
 
-                @pl.when(valid | (pos == c))
-                def _():
-                    pass_on(0, zof(pos), y, side)
+                @pl.when((valid & onward[side]) | ((pos == c) & own_onward[side]))
+                def _():
+                    forward(0, zof(pos), y, side).start()
+
+                @pl.when(valid & ~onward[side])
+                def _():
+                    landed(1, zof(pos), y)
 
         def side_step(side, _):
             pos = jnp.where(side == 2, c, jnp.where(side == 0, x_l, x_r))
@@ -373,13 +423,22 @@
                 else:
                     go_home(pb, z, y).start()
 
-        @pl.when(j == last - 1)
+        @pl.when(j == jnp.where(inner, X_LAST - 2, X_LAST - 1))
         def _():
             lax.fori_loop(other * per_half, (other + 1) * per_half, grads_in, None)
             send_in.start()
+
+        @pl.when(j == jnp.where(inner, X_LAST - 2, X_LAST - 1))
+        def _():
             lax.fori_loop(other * per_half, (other + 1) * per_half, grads_down, None)
             send_down.start()
+
+        @pl.when(j == jnp.where(inner, X_LAST - 2, X_LAST - 1))
+        def _():
             lax.fori_loop(rep * per_half, (rep + 1) * per_half, grads_in, None)
+
+        @pl.when(j == jnp.where(inner, X_LAST - 2, X_LAST - 1))
+        def _():
             lax.fori_loop(rep * per_half, (rep + 1) * per_half, grads_down, None)
 
     lax.fori_loop(0, STEPS, step, None)
@@ -414,12 +473,18 @@
     for e in range(EXPERTS):
         remote(f_out.at[e], f_out.at[e], rsend.at[0, 0], fr.at[e], twin).wait_recv()
 
-    for e in range(EXPERTS):
-        entry(e, 0).wait_send()
-
-        @pl.when(mine != e)
-        def _():
-            entry(e, 1).wait_send()
+    for t in range(2):
+        entries(t, 0, lambda copy: copy.wait_send())
+
+        @pl.when(at_end)
+        def _():
+            entries(t, 1, lambda copy: copy.wait_send())
+
+    @pl.when(inner)
+    def _():
+        for copy in raw_copies:
+            copy.wait_send()
+
     for i, (src, dst) in enumerate(w_parts):
         remote(src, dst(rows), wsend.at[i], wrecv.at[i], twin).wait_send()
     send_target.wait_send()
@@ -437,10 +502,10 @@
                 copy().wait_send()
 
         for y in halves:
-            sent((z_in_left | (j == 0)) & (c < 3), lambda: forward(1, zof(z_l), y, 1))
-            sent((z_in_right | (j == 0)) & (c > 0), lambda: forward(1, zof(z_r), y, 0))
-            sent((x_in_left | (x_l == c)) & (c < 3), lambda: forward(0, zof(x_l), y, 1))
-            sent((x_in_right | (x_r == c)) & (c > 0), lambda: forward(0, zof(x_r), y, 0))
+            sent((z_in_left & onward[1]) | ((j == 0) & own_onward[1]), lambda: forward(1, zof(z_l), y, 1))
+            sent((z_in_right & onward[0]) | ((j == 0) & own_onward[0]), lambda: forward(1, zof(z_r), y, 0))
+            sent((x_in_left & onward[1]) | ((x_l == c) & own_onward[1]), lambda: forward(0, zof(x_l), y, 1))
+            sent((x_in_right & onward[0]) | ((x_r == c) & own_onward[0]), lambda: forward(0, zof(x_r), y, 0))
             sent(x_in_left & (c == 3), lambda: go_back(pb, zof(x_l), y, 0, False))
             sent(x_in_right & (c == 0), lambda: go_back(pb, zof(x_r), y, 1, False))
             sent(from_right & (b_r < c) & (c > 0), lambda: go_back(rb, zof(b_r), y, 0, False))
@@ -484,6 +549,9 @@
         scratch_shapes=[
             pltpu.VMEM((EXPERTS, CAP, width), BF16),
             pltpu.VMEM((EXPERTS, CAP, width), BF16),
+            pltpu.VMEM((2, EXPERTS, CAP, width), BF16),
+            pltpu.VMEM((2, tokens, width), BF16),
+            pltpu.VMEM((8, tokens), jnp.int32),
             pltpu.VMEM((8, tokens), jnp.int32),
             pltpu.VMEM((8, tokens), jnp.int32),
             pltpu.VMEM((RING, 2, CAP, width), BF16),
@@ -497,8 +565,10 @@
             pltpu.VMEM((half, 2 * units), BF16),
             pltpu.VMEM((units, half), BF16),
             dma((2,)),
+            dma((3,)),
+            dma((3,)),
             dma((2, RING, 2)),
-            dma((2, EXPERTS)),
+            dma((2, 2, EXPERTS)),
             dma((2, 2, RING, 2)),
             dma((RING + 1, 2)),
             dma((RING, 2)),

time: 295 us -> 286 us (0.969)
  the two profiles are of different devices: /device:TPU:30 before, /device:TPU:56 now
where the time goes in v4:
time: 286 us
  Pallas kernels  286 us (100%)
    pallas_call x1, Pallas kernels, body(): pl.pallas_call(kernel, out_shape=(jax.ShapeDtypeStruct((EXPERTS, CAP, wid...  281 us

profile of v4, /device:TPU:56, one launch (start us, length us, event | category | flops | bytes accessed | tf_op | source)
XLA Modules:
  0.0 286.2 jit_solution(5248211941701811517)
XLA Ops:
  0.6 280.7 %shard_map.102 = (bf16[4,48,4096]{2,1,0:T(8,128)(2,1)}, bf16[2048,384]{1,0:T(8,128)(2,1)}, bf16[2048,384]{1,0:T(8,128)(2,1)}, bf16[384,2048]{1,0:T(8,128)(2,1)}) custom-call(bf16[128,4096]{1,0:T(8,128)(2,1)} %bitcast.16, bf16[128,4096]{1,0:T(8,128)(2,1)} %bitcast.17, f32[1,128]{1,0:T(1,128)} %bitcast.20, s32[1,128]{1,0:T(1,128)} %bitcast.18, ...), custom_call_target="tpu_custom_call" | custom-call | tf_op jit(solution)/shard_map/pallas_call | solution.py:544
  281.3 4.9 %shard_map.103 = (bf16[128,4096]{1,0:T(8,128)(2,1)}, bf16[2048,384]{1,0:T(8,128)(2,1)}, bf16[2048,384]{1,0:T(8,128)(2,1)}, bf16[384,2048]{1,0:T(8,128)(2,1)}) custom-call(bf16[192,4096]{1,0:T(8,128)(2,1)} %bitcast.15, s32[1,128]{1,0:T(1,128)} %bitcast.19, bf16[2048,384]{1,0:T(8,128)(2,1)} %get-tuple-element.13.gg, bf16[2048,384]{1,0:T(8,128)(2,1)} %get-tuple-element.14.gu, ...), custom_call_target="tpu_custom_call" | custom-call | tf_op jit(solution)/shard_map/pallas_call | solution.py:591

commit v5 on v4

--- a/solution.py
+++ b/solution.py
@@ -470,9 +470,6 @@
     lax.fori_loop(0, half // piece, add_down, None)
     outs[2].start()
 
-    for e in range(EXPERTS):
-        remote(f_out.at[e], f_out.at[e], rsend.at[0, 0], fr.at[e], twin).wait_recv()
-
     for t in range(2):
         entries(t, 0, lambda copy: copy.wait_send())
 
@@ -515,6 +512,8 @@
 
     lax.fori_loop(0, STEPS, drain, None)
     go_home(pb, z, 1 - yh).wait_send()
+    for e in range(EXPERTS):
+        remote(f_out.at[e], f_out.at[e], rsend.at[0, 0], fr.at[e], twin).wait_recv()
     for out in outs:
         out.wait()
 

time: 286 us -> 285 us (level)
  the two profiles are of different devices: /device:TPU:56 before, /device:TPU:40 now
where the time goes in v5:
time: 285 us
  Pallas kernels  284 us (100%)
    pallas_call x1, Pallas kernels, body(): pl.pallas_call(kernel, out_shape=(jax.ShapeDtypeStruct((EXPERTS, CAP, wid...  279 us

profile of v5, /device:TPU:40, one launch (start us, length us, event | category | flops | bytes accessed | tf_op | source)
XLA Modules:
  0.0 284.9 jit_solution(14901107031294656598)
XLA Ops:
  0.6 279.4 %shard_map.102 = (bf16[4,48,4096]{2,1,0:T(8,128)(2,1)}, bf16[2048,384]{1,0:T(8,128)(2,1)}, bf16[2048,384]{1,0:T(8,128)(2,1)}, bf16[384,2048]{1,0:T(8,128)(2,1)}) custom-call(bf16[128,4096]{1,0:T(8,128)(2,1)} %bitcast.16, bf16[128,4096]{1,0:T(8,128)(2,1)} %bitcast.17, f32[1,128]{1,0:T(1,128)} %bitcast.20, s32[1,128]{1,0:T(1,128)} %bitcast.18, ...), custom_call_target="tpu_custom_call" | custom-call | tf_op jit(solution)/shard_map/pallas_call | solution.py:543
  280.0 4.9 %shard_map.103 = (bf16[128,4096]{1,0:T(8,128)(2,1)}, bf16[2048,384]{1,0:T(8,128)(2,1)}, bf16[2048,384]{1,0:T(8,128)(2,1)}, bf16[384,2048]{1,0:T(8,128)(2,1)}) custom-call(bf16[192,4096]{1,0:T(8,128)(2,1)} %bitcast.15, s32[1,128]{1,0:T(1,128)} %bitcast.19, bf16[2048,384]{1,0:T(8,128)(2,1)} %get-tuple-element.13.gg, bf16[2048,384]{1,0:T(8,128)(2,1)} %get-tuple-element.14.gu, ...), custom_call_target="tpu_custom_call" | custom-call | tf_op jit(solution)/shard_map/pallas_call | solution.py:590
